TPU v7x, 32 devices: a whole 2x2x4 slice. The times are simulated.
32 devices in a mesh: edp: 4 (over x, core), ep: 8 (over z, y).
Axes of the slice: x: 2, y: 2, z: 4, core: 2. Of those that a mesh axis runs over, the one named last changes fastest.
Arguments:
- tokens: bfloat16 [4096, 5120], P(('edp', 'ep')), may hold values from -6 to 6
- cotangent: bfloat16 [4096, 5120], P(('edp', 'ep')), may hold values from -4 to 4
- gate_probs: bfloat16 [4096, 6], P(('edp', 'ep')), may hold values from 0.099609375 to 1
- expert_ids: int32 [4096, 6], P(('edp', 'ep')), may hold values from 0 to 159, all different within a row
- w_gate: bfloat16 [8, 1536, 5120], P('ep', 'edp'), may hold values from -0.078125 to 0.078125
- w_up: bfloat16 [8, 1536, 5120], P('ep', 'edp'), may hold values from -0.078125 to 0.078125
- w_down: bfloat16 [8, 1536, 5120], P('ep', 'edp'), may hold values from -0.15625 to 0.15625
Outputs:
- token_grad: bfloat16 [4096, 5120], P(('edp', 'ep'))
- gate_grad: bfloat16 [4096, 6], P(('edp', 'ep'))
- gate_wgrad: bfloat16 [8, 1536, 5120], P('ep', 'edp')
- up_wgrad: bfloat16 [8, 1536, 5120], P('ep', 'edp')
- down_wgrad: bfloat16 [8, 1536, 5120], P('ep', 'edp')
Inputs may be any that keep to these rules, and one draw needn't show every extreme that they name: `expert_ids`: each row holds 6 different ids, and every id appears in some row.
All inputs are finite; a program needn't handle non-finite values.
Results may differ from a plain program's by a relative error of at most 0.008.
Values may be sent and summed in bfloat16 or wider, within the bound.
A program may use at most 128 MiB of HBM per device.

v0:
```python
import jax
import jax.numpy as jnp
from jax import lax
from jax.sharding import PartitionSpec as P

EXP_EP = 1
CAP = 3


def route_tables(expert_ids, experts, capacity):
    tok_count = expert_ids.shape[0]
    matches = (
        expert_ids[:, :, None] == jnp.arange(experts, dtype=jnp.int32)[None, None, :]
    ).astype(jnp.float32)
    counts = jnp.sum(matches, axis=1)
    positions = jnp.arange(tok_count, dtype=jnp.int32)
    earlier = (positions[None, :] < positions[:, None]).astype(jnp.float32)
    before = jnp.dot(earlier, counts, precision=lax.Precision.HIGHEST)
    slot_pos = jnp.sum(matches * before[:, None, :], axis=2)
    column = expert_ids.astype(jnp.float32) * capacity + slot_pos
    inside = (expert_ids < experts) & (slot_pos < capacity)
    targets = jnp.arange(experts * capacity, dtype=jnp.float32)
    hits = inside[:, :, None] & (column[:, :, None] == targets[None, None, :])
    return jnp.where(hits, 1.0, 0.0).astype(jnp.float32)


def forward_part(all_x, gate_mat, up_mat, model_width):
    x_rows = all_x.reshape(-1, model_width)
    contract = (((1,), (1,)), ((), ()))
    pre_gate = lax.dot_general(x_rows, gate_mat, contract, preferred_element_type=jnp.float32)
    pre_up = lax.dot_general(x_rows, up_mat, contract, preferred_element_type=jnp.float32)
    return (x_rows, pre_gate, pre_up)


def spread_rows(received, ep_size, capacity, split):
    tail = received.shape[2:]
    grouped = received.reshape((ep_size, EXP_EP, capacity) + tail)
    order = (1, 0) + tuple(range(2, grouped.ndim))
    return jnp.repeat(grouped.transpose(order), split, axis=0)


def per_device(tokens, cotangent, gate_probs, expert_ids, w_gate, w_up, w_down):
    edp_size = lax.axis_size("edp")
    ep_size = lax.axis_size("ep")
    split = edp_size // EXP_EP
    experts = EXP_EP * ep_size
    model_width = tokens.shape[1]
    capacity = CAP
    tables = route_tables(expert_ids, experts, capacity)
    route_matrix = jnp.sum(tables, axis=1).astype(jnp.bfloat16)
    send_x = jnp.einsum("tc,td->cd", route_matrix, tokens, preferred_element_type=jnp.float32)
    send_x = send_x.astype(jnp.bfloat16).reshape(ep_size, EXP_EP * capacity, model_width)
    send_dy = jnp.einsum("tc,td->cd", route_matrix, cotangent, preferred_element_type=jnp.float32)
    send_dy = send_dy.astype(jnp.bfloat16).reshape(ep_size, EXP_EP * capacity, model_width)
    send_p = jnp.einsum("trc,tr->c", tables, gate_probs.astype(jnp.float32))
    send_p = send_p.astype(jnp.bfloat16).reshape(ep_size, EXP_EP * capacity)
    recv_x, recv_dy, recv_p = (
        lax.all_to_all(send_x, "ep", split_axis=0, concat_axis=0, tiled=True),
        lax.all_to_all(send_dy, "ep", split_axis=0, concat_axis=0, tiled=True),
        lax.all_to_all(send_p, "ep", split_axis=0, concat_axis=0, tiled=True),
    )
    spread_x = spread_rows(recv_x, ep_size, capacity, split)
    spread_dy = spread_rows(recv_dy, ep_size, capacity, split)
    spread_p = spread_rows(recv_p, ep_size, capacity, split)
    gate_mat = w_gate[0]
    up_mat = w_up[0]
    down_mat = w_down[0]
    all_x, all_dy, all_p = (
        lax.all_to_all(spread_x, "edp", split_axis=0, concat_axis=0, tiled=True),
        lax.all_to_all(spread_dy, "edp", split_axis=0, concat_axis=0, tiled=True),
        lax.all_to_all(spread_p, "edp", split_axis=0, concat_axis=0, tiled=True),
    )
    x_rows, pre_gate, pre_up = forward_part(all_x, gate_mat, up_mat, model_width)
    dy_rows = all_dy.reshape(-1, model_width)
    prob_col = all_p.reshape(-1).astype(jnp.float32)[:, None]
    sigma_gate = jax.nn.sigmoid(pre_gate)
    hidden = pre_gate * sigma_gate * pre_up
    contract = (((1,), (1,)), ((), ()))
    back_hid = lax.dot_general(dy_rows, down_mat, contract, preferred_element_type=jnp.float32)
    slot_part = jnp.sum(hidden * back_hid, axis=1)
    grad_hid = prob_col * back_hid
    grad_gate = (grad_hid * pre_up * sigma_gate * (1.0 + pre_gate * (1.0 - sigma_gate))).astype(
        jnp.bfloat16
    )
    grad_up = (grad_hid * pre_gate * sigma_gate).astype(jnp.bfloat16)
    scaled_cot = (prob_col * dy_rows.astype(jnp.float32)).astype(jnp.bfloat16)
    hidden_half = hidden.astype(jnp.bfloat16)
    outer = (((0,), (0,)), ((), ()))
    down_wgrad = lax.dot_general(
        hidden_half, scaled_cot, outer, preferred_element_type=jnp.float32
    ).astype(jnp.bfloat16)
    gate_wgrad = lax.dot_general(
        grad_gate, x_rows, outer, preferred_element_type=jnp.float32
    ).astype(jnp.bfloat16)
    up_wgrad = lax.dot_general(grad_up, x_rows, outer, preferred_element_type=jnp.float32).astype(
        jnp.bfloat16
    )
    partial_sum = jnp.dot(grad_gate, gate_mat, preferred_element_type=jnp.float32)
    partial_sum = partial_sum + jnp.dot(grad_up, up_mat, preferred_element_type=jnp.float32)
    partial_half = partial_sum.astype(jnp.bfloat16).reshape(
        edp_size, ep_size * capacity, model_width
    )
    came_dx = lax.all_to_all(partial_half, "edp", split_axis=0, concat_axis=0, tiled=True)
    summed_dx = jnp.sum(
        came_dx.reshape(EXP_EP, split, ep_size * capacity, model_width).astype(jnp.float32), axis=1
    )
    slot_dx = (
        summed_dx.reshape(EXP_EP, ep_size, capacity, model_width)
        .transpose(1, 0, 2, 3)
        .astype(jnp.bfloat16)
    )
    came_dp = lax.all_to_all(
        slot_part.reshape(edp_size, ep_size * capacity),
        "edp",
        split_axis=0,
        concat_axis=0,
        tiled=True,
    )
    summed_dp = jnp.sum(came_dp.reshape(EXP_EP, split, ep_size, capacity), axis=1)
    slot_gp = summed_dp.transpose(1, 0, 2).astype(jnp.bfloat16)
    back_x, back_p = (
        lax.all_to_all(slot_dx, "ep", split_axis=0, concat_axis=0, tiled=True),
        lax.all_to_all(slot_gp, "ep", split_axis=0, concat_axis=0, tiled=True),
    )
    token_grad = jnp.dot(
        route_matrix,
        back_x.reshape(experts * capacity, model_width),
        preferred_element_type=jnp.float32,
    ).astype(jnp.bfloat16)
    gate_grad = jnp.einsum("trc,c->tr", tables, back_p.reshape(-1).astype(jnp.float32)).astype(
        jnp.bfloat16
    )
    return (token_grad, gate_grad, gate_wgrad[None], up_wgrad[None], down_wgrad[None])


def solution(mesh):
    in_specs = (
        P(("edp", "ep"), None),
        P(("edp", "ep"), None),
        P(("edp", "ep"), None),
        P(("edp", "ep"), None),
        P("ep", "edp", None),
        P("ep", "edp", None),
        P("ep", "edp", None),
    )
    out_specs = (
        P(("edp", "ep"), None),
        P(("edp", "ep"), None),
        P("ep", "edp", None),
        P("ep", "edp", None),
        P("ep", "edp", None),
    )
    return jax.shard_map(
        per_device, mesh=mesh, in_specs=in_specs, out_specs=out_specs, check_vma=False
    )
```

profile of v0, /device:TPU:0, one launch (start us, length us, event | category | flops | bytes accessed | tf_op | source)
XLA Modules:
  0.0 154.8 jit_solution(966578852100021795)
XLA Ops:
  5.2 7.3 %all-to-all-start = ((bf16[8,1,3]{2,1,0:T(2,128)(2,1)}), bf16[8,1,3]{2,1,0:T(2,128)(2,1)S(1)}, u32[]{:S(2)}, u32[]{:S(2)}) async-start(bf16[8,1,3]{2,1,0:T(2,128)(2,1)} %all_to_all.51), calls=%async_computation | async-start | bytes 8192 | tf_op jit(solution)/shard_map/all_to_all | solution.py:60
  12.5 6.4 %all-to-all-done = bf16[8,1,3]{2,1,0:T(2,128)(2,1)S(1)} async-done(((bf16[8,1,3]{2,1,0:T(2,128)(2,1)}), bf16[8,1,3]{2,1,0:T(2,128)(2,1)S(1)}, u32[]{:S(2)}, u32[]{:S(2)}) %all-to-all-start) | async-done | bytes 80 | tf_op jit(solution)/shard_map/all_to_all | solution.py:60
  19.6 3.2 %all-to-all-start.1 = ((bf16[4,8,3]{1,2,0:T(4,128)(2,1)}), bf16[4,8,3]{1,2,0:T(4,128)(2,1)S(1)}, u32[]{:S(2)}, u32[]{:S(2)}) async-start(bf16[4,8,3]{1,2,0:T(4,128)(2,1)} %reshape.95), calls=%async_computation.1 | async-start | bytes 8192 | tf_op jit(solution)/shard_map/all_to_all | solution.py:71
  24.0 2.6 %all-to-all-done.1 = bf16[4,8,3]{1,2,0:T(4,128)(2,1)S(1)} async-done(((bf16[4,8,3]{1,2,0:T(4,128)(2,1)}), bf16[4,8,3]{1,2,0:T(4,128)(2,1)S(1)}, u32[]{:S(2)}, u32[]{:S(2)}) %all-to-all-start.1) | async-done | bytes 224 | tf_op jit(solution)/shard_map/all_to_all | solution.py:71
  26.6 3.4 %all-to-all-start.2 = ((bf16[8,3,5120]{2,1,0:T(4,128)(2,1)}), bf16[8,3,5120]{2,1,0:T(4,128)(2,1)S(1)}, u32[]{:S(2)}, u32[]{:S(2)}) async-start(bf16[8,3,5120]{2,1,0:T(4,128)(2,1)} %reshape.96), calls=%async_computation.2 | async-start | bytes 655360 | tf_op jit(solution)/shard_map/all_to_all | solution.py:59
  30.1 1.6 %convolution_convert_fusion.4 = bf16[24,5120]{1,0:T(8,128)(2,1)S(1)} fusion(bf16[128,5120]{1,0:T(8,128)(2,1)} %param.7, bf16[128,24]{0,1:T(8,128)(2,1)S(1)} %select_reduce_fusion), kind=kOutput, calls=%fused_computation.9 | convolution fusion | flops 31580160 | bytes 1562624 | tf_op jit(solution)/shard_map/tc,td->cd/dot_general | solution.py:51
  32.5 7.9 %all-to-all-done.2 = bf16[8,3,5120]{2,1,0:T(4,128)(2,1)S(1)} async-done(((bf16[8,3,5120]{2,1,0:T(4,128)(2,1)}), bf16[8,3,5120]{2,1,0:T(4,128)(2,1)S(1)}, u32[]{:S(2)}, u32[]{:S(2)}) %all-to-all-start.2) | async-done | bytes 245792 | tf_op jit(solution)/shard_map/all_to_all | solution.py:59
  40.5 3.6 %all-to-all-start.4 = ((bf16[8,3,5120]{2,1,0:T(4,128)(2,1)}), bf16[8,3,5120]{2,1,0:T(4,128)(2,1)S(1)}, u32[]{:S(2)}, u32[]{:S(2)}) async-start(bf16[8,3,5120]{2,1,0:T(4,128)(2,1)} %reshape.99), calls=%async_computation.4 | async-start | bytes 655360 | tf_op jit(solution)/shard_map/all_to_all | solution.py:58
  44.2 10.2 %all-to-all-done.4 = bf16[8,3,5120]{2,1,0:T(4,128)(2,1)S(1)} async-done(((bf16[8,3,5120]{2,1,0:T(4,128)(2,1)}), bf16[8,3,5120]{2,1,0:T(4,128)(2,1)S(1)}, u32[]{:S(2)}, u32[]{:S(2)}) %all-to-all-start.4) | async-done | bytes 245792 | tf_op jit(solution)/shard_map/all_to_all | solution.py:58
  55.4 3.5 %all-to-all-start.3 = ((bf16[4,8,3,5120]{3,1,2,0:T(8,128)(2,1)}), bf16[4,8,3,5120]{3,1,2,0:T(8,128)(2,1)S(1)}, u32[]{:S(2)}, u32[]{:S(2)}) async-start(bf16[4,8,3,5120]{3,1,2,0:T(8,128)(2,1)} %reshape.97), calls=%async_computation.3 | async-start | bytes 1966080 | tf_op jit(solution)/shard_map/all_to_all | solution.py:70
  59.1 13.6 %all-to-all-done.3 = bf16[4,8,3,5120]{3,1,2,0:T(8,128)(2,1)S(1)} async-done(((bf16[4,8,3,5120]{3,1,2,0:T(8,128)(2,1)}), bf16[4,8,3,5120]{3,1,2,0:T(8,128)(2,1)S(1)}, u32[]{:S(2)}, u32[]{:S(2)}) %all-to-all-start.3) | async-done | bytes 983072 | tf_op jit(solution)/shard_map/all_to_all | solution.py:70
  73.7 3.5 %all-to-all-start.5 = ((bf16[4,8,3,5120]{3,1,2,0:T(8,128)(2,1)}), bf16[4,8,3,5120]{3,1,2,0:T(8,128)(2,1)S(1)}, u32[]{:S(2)}, u32[]{:S(2)}) async-start(bf16[4,8,3,5120]{3,1,2,0:T(8,128)(2,1)} %reshape.100), calls=%async_computation.5 | async-start | bytes 1966080 | tf_op jit(solution)/shard_map/all_to_all | solution.py:69
  77.5 1.9 %copy.53 = bf16[4,8,3,5120]{3,2,1,0:T(4,128)(2,1)} copy(bf16[4,8,3,5120]{3,1,2,0:T(8,128)(2,1)S(1)} %all-to-all-done.3) | data formatting | bytes 1966080 | tf_op jit(solution)/shard_map/all_to_all | solution.py:70
  79.4 1.9 %reshape.98 = bf16[96,5120]{1,0:T(8,128)(2,1)S(1)} reshape(bf16[4,8,3,5120]{3,2,1,0:T(4,128)(2,1)} %copy.53) | data formatting | bytes 1966080 | tf_op jit(solution)/shard_map/reshape | solution.py:74
  81.3 9.7 %all-to-all-done.5 = bf16[4,8,3,5120]{3,1,2,0:T(8,128)(2,1)S(1)} async-done(((bf16[4,8,3,5120]{3,1,2,0:T(8,128)(2,1)}), bf16[4,8,3,5120]{3,1,2,0:T(8,128)(2,1)S(1)}, u32[]{:S(2)}, u32[]{:S(2)}) %all-to-all-start.5) | async-done | bytes 983072 | tf_op jit(solution)/shard_map/all_to_all | solution.py:69
  91.0 1.9 %copy.55 = bf16[4,8,3,5120]{3,2,1,0:T(4,128)(2,1)} copy(bf16[4,8,3,5120]{3,1,2,0:T(8,128)(2,1)S(1)} %all-to-all-done.5) | data formatting | bytes 1966080 | tf_op jit(solution)/shard_map/all_to_all | solution.py:69
  92.9 1.9 %reshape.101 = bf16[96,5120]{1,0:T(8,128)(2,1)S(1)} reshape(bf16[4,8,3,5120]{3,2,1,0:T(4,128)(2,1)} %copy.55) | data formatting | bytes 1966080 | tf_op jit(solution)/shard_map/reshape | solution.py:28
  94.8 3.6 %fusion.6 = f32[96,384]{1,0:T(8,128)S(1)} fusion(bf16[96,5120]{1,0:T(8,128)(2,1)S(1)} %reshape.101, bf16[1,384,5120]{2,1,0:T(8,128)(2,1)} %param.11), kind=kOutput, calls=%fused_computation.13 | convolution fusion | flops 377487360 | bytes 5062656 | tf_op jit(solution)/shard_map/dot_general | solution.py:30
  99.7 2.1 %multiply_reduce_fusion = (f32[96]{0:T(128)S(1)}, bf16[96,384]{1,0:T(8,128)(2,1)S(1)}, bf16[96,384]{1,0:T(8,128)(2,1)}) fusion(f32[96,384]{1,0:T(8,128)S(1)} %fusion.9, f32[96,384]{1,0:T(8,128)S(1)} %fusion.6, f32[96]{0:T(128)S(1)} %reshape.105, bf16[96,5120]{1,0:T(8,128)(2,1)S(1)} %reshape.98, bf16[1,384,5120]{2,1,0:T(8,128)(2,1)S(1)} %copy-done.3), kind=kOutput, calls=%fused_computation.24 | convolution fusion | flops 378150816 | bytes 5358336 | tf_op jit(solution)/shard_map/dot_general | solution.py:79
  102.5 3.2 %all-to-all-start.8 = ((f32[4,1,24]{2,1,0:T(1,128)}), f32[4,1,24]{2,1,0:T(1,128)S(1)}, u32[]{:S(2)}, u32[]{:S(2)}) async-start(f32[4,1,24]{2,1,0:T(1,128)} %bitcast.8), calls=%async_computation.8 | async-start | bytes 4096 | tf_op jit(solution)/shard_map/all_to_all | solution.py:112
  105.7 3.1 %fusion.4 = f32[96,5120]{1,0:T(8,128)S(1)} fusion(bf16[96,384]{1,0:T(8,128)(2,1)S(1)} %get-tuple-element.6, bf16[1,384,5120]{2,1,0:T(8,128)(2,1)} %param.11), kind=kOutput, calls=%fused_computation.11 | convolution fusion | flops 377487360 | bytes 5971968 | tf_op jit(solution)/shard_map/dot_general | solution.py:98
  109.0 1.8 %fusion.3 = bf16[96,5120]{1,0:T(8,128)(2,1)} fusion(f32[96,5120]{1,0:T(8,128)S(1)} %fusion.4, bf16[96,384]{1,0:T(8,128)(2,1)S(1)} %copy-done.6, bf16[1,384,5120]{2,1,0:T(8,128)(2,1)S(1)} %copy-done.2), kind=kOutput, calls=%fused_computation.8 | convolution fusion | flops 378470400 | bytes 6955008 | tf_op jit(solution)/shard_map/dot_general | solution.py:99
  110.8 4.2 %all-to-all-start.6 = ((bf16[4,24,5120]{2,1,0:T(8,128)(2,1)}), bf16[4,24,5120]{2,1,0:T(8,128)(2,1)}, u32[]{:S(2)}, u32[]{:S(2)}) async-start(bf16[4,24,5120]{2,1,0:T(8,128)(2,1)} %bitcast.50), calls=%async_computation.6 | async-start | bytes 1966080 | tf_op jit(solution)/shard_map/all_to_all | solution.py:103
  115.1 4.0 %fusion.1 = bf16[1,384,5120]{2,1,0:T(8,128)(2,1)} fusion(bf16[96,384]{1,0:T(8,128)(2,1)} %get-tuple-element.7, bf16[96,5120]{1,0:T(8,128)(2,1)S(1)} %reshape.101), kind=kOutput, calls=%fused_computation.4 | convolution fusion | flops 379453440 | bytes 4988928 | tf_op jit(solution)/shard_map/dot_general | solution.py:95
  119.8 9.1 %all-to-all-done.6 = bf16[4,24,5120]{2,1,0:T(8,128)(2,1)} async-done(((bf16[4,24,5120]{2,1,0:T(8,128)(2,1)}), bf16[4,24,5120]{2,1,0:T(8,128)(2,1)}, u32[]{:S(2)}, u32[]{:S(2)}) %all-to-all-start.6) | async-done | bytes 983072 | tf_op jit(solution)/shard_map/all_to_all | solution.py:103
  128.9 3.6 %all-to-all-start.9 = ((bf16[8,1,3]{2,1,0:T(2,128)(2,1)}), bf16[8,1,3]{2,1,0:T(2,128)(2,1)S(1)}, u32[]{:S(2)}, u32[]{:S(2)}) async-start(bf16[8,1,3]{2,1,0:T(2,128)(2,1)} %convert_element_type.115), calls=%async_computation.9 | async-start | bytes 8192 | tf_op jit(solution)/shard_map/all_to_all | solution.py:123
  132.5 2.1 %reduce_sum.60 = bf16[24,5120]{1,0:T(8,128)(2,1)} reduce(bf16[4,24,5120]{2,1,0:T(8,128)(2,1)} %all-to-all-done.6, bf16[]{:T(256)} %constant.11.clone.1), dimensions={0}, to_apply=%region_3.4 | reduce | flops 368640 | bytes 1228802 | tf_op jit(solution)/shard_map/reduce_sum | solution.py:104
  134.6 1.8 %convert_element_type.103 = bf16[8,1,3,5120]{3,2,0,1:T(4,128)(2,1)} reshape(bf16[24,5120]{1,0:T(8,128)(2,1)} %reduce_sum.60) | data formatting | bytes 491520 | tf_op jit(solution)/shard_map/convert_element_type | solution.py:110
  136.4 2.5 %all-to-all-done.9 = bf16[8,1,3]{2,1,0:T(2,128)(2,1)S(1)} async-done(((bf16[8,1,3]{2,1,0:T(2,128)(2,1)}), bf16[8,1,3]{2,1,0:T(2,128)(2,1)S(1)}, u32[]{:S(2)}, u32[]{:S(2)}) %all-to-all-start.9) | async-done | bytes 80 | tf_op jit(solution)/shard_map/all_to_all | solution.py:123
  138.9 4.2 %all-to-all-start.7 = ((bf16[8,1,3,5120]{3,2,1,0:T(4,128)(2,1)}), bf16[8,1,3,5120]{3,2,1,0:T(4,128)(2,1)}, u32[]{:S(2)}, u32[]{:S(2)}) async-start(bf16[8,1,3,5120]{3,2,1,0:T(4,128)(2,1)} %bitcast.51), calls=%async_computation.7 | async-start | bytes 655360 | tf_op jit(solution)/shard_map/all_to_all | solution.py:122
  143.1 3.1 %fusion = bf16[1,384,5120]{2,1,0:T(8,128)(2,1)} fusion(bf16[96,384]{1,0:T(8,128)(2,1)S(1)} %get-tuple-element.6, bf16[96,5120]{1,0:T(8,128)(2,1)S(1)} %reshape.101), kind=kOutput, calls=%fused_computation.3 | convolution fusion | flops 379453440 | bytes 4988928 | tf_op jit(solution)/shard_map/dot_general | solution.py:92
  146.3 3.2 %fusion.2 = bf16[1,384,5120]{2,1,0:T(8,128)(2,1)} fusion(bf16[96,5120]{1,0:T(8,128)(2,1)S(1)} %reshape.98, f32[96]{0:T(128)S(1)} %reshape.105, f32[96,384]{1,0:T(8,128)S(1)} %copy-done.5, f32[96,384]{1,0:T(8,128)S(1)} %fusion.6), kind=kOutput, calls=%fused_computation.5 | convolution fusion | flops 381149184 | bytes 5210496 | tf_op jit(solution)/shard_map/dot_general | solution.py:89
  (46 shorter events, 18.1 us)
Async XLA Ops:
  0.6 22.2 %copy-start = (bf16[128,5120]{1,0:T(8,128)(2,1)S(1)}, bf16[128,5120]{1,0:T(8,128)(2,1)}, u32[]{:S(2)}) copy-start(bf16[128,5120]{1,0:T(8,128)(2,1)} %param.8) | copy-start | bytes 3932164
  5.2 13.7 %all-to-all-start = ((bf16[8,1,3]{2,1,0:T(2,128)(2,1)}), bf16[8,1,3]{2,1,0:T(2,128)(2,1)S(1)}, u32[]{:S(2)}, u32[]{:S(2)}) async-start(bf16[8,1,3]{2,1,0:T(2,128)(2,1)} %all_to_all.51), calls=%async_computation | async-start | bytes 8192 | tf_op jit(solution)/shard_map/all_to_all | solution.py:60
  19.6 7.0 %all-to-all-start.1 = ((bf16[4,8,3]{1,2,0:T(4,128)(2,1)}), bf16[4,8,3]{1,2,0:T(4,128)(2,1)S(1)}, u32[]{:S(2)}, u32[]{:S(2)}) async-start(bf16[4,8,3]{1,2,0:T(4,128)(2,1)} %reshape.95), calls=%async_computation.1 | async-start | bytes 8192 | tf_op jit(solution)/shard_map/all_to_all | solution.py:71
  26.6 13.9 %all-to-all-start.2 = ((bf16[8,3,5120]{2,1,0:T(4,128)(2,1)}), bf16[8,3,5120]{2,1,0:T(4,128)(2,1)S(1)}, u32[]{:S(2)}, u32[]{:S(2)}) async-start(bf16[8,3,5120]{2,1,0:T(4,128)(2,1)} %reshape.96), calls=%async_computation.2 | async-start | bytes 655360 | tf_op jit(solution)/shard_map/all_to_all | solution.py:59
  40.5 13.9 %all-to-all-start.4 = ((bf16[8,3,5120]{2,1,0:T(4,128)(2,1)}), bf16[8,3,5120]{2,1,0:T(4,128)(2,1)S(1)}, u32[]{:S(2)}, u32[]{:S(2)}) async-start(bf16[8,3,5120]{2,1,0:T(4,128)(2,1)} %reshape.99), calls=%async_computation.4 | async-start | bytes 655360 | tf_op jit(solution)/shard_map/all_to_all | solution.py:58
  55.4 17.2 %all-to-all-start.3 = ((bf16[4,8,3,5120]{3,1,2,0:T(8,128)(2,1)}), bf16[4,8,3,5120]{3,1,2,0:T(8,128)(2,1)S(1)}, u32[]{:S(2)}, u32[]{:S(2)}) async-start(bf16[4,8,3,5120]{3,1,2,0:T(8,128)(2,1)} %reshape.97), calls=%async_computation.3 | async-start | bytes 1966080 | tf_op jit(solution)/shard_map/all_to_all | solution.py:70
  73.7 17.2 %all-to-all-start.5 = ((bf16[4,8,3,5120]{3,1,2,0:T(8,128)(2,1)}), bf16[4,8,3,5120]{3,1,2,0:T(8,128)(2,1)S(1)}, u32[]{:S(2)}, u32[]{:S(2)}) async-start(bf16[4,8,3,5120]{3,1,2,0:T(8,128)(2,1)} %reshape.100), calls=%async_computation.5 | async-start | bytes 1966080 | tf_op jit(solution)/shard_map/all_to_all | solution.py:69
  94.8 3.6 %copy-start.1 = (bf16[1,384,5120]{2,1,0:T(8,128)(2,1)S(1)}, bf16[1,384,5120]{2,1,0:T(8,128)(2,1)}, u32[]{:S(2)}) copy-start(bf16[1,384,5120]{2,1,0:T(8,128)(2,1)} %param.12) | copy-start | bytes 11796484
  94.8 4.9 %copy-start.3 = (bf16[1,384,5120]{2,1,0:T(8,128)(2,1)S(1)}, bf16[1,384,5120]{2,1,0:T(8,128)(2,1)}, u32[]{:S(2)}) copy-start(bf16[1,384,5120]{2,1,0:T(8,128)(2,1)} %param.13) | copy-start | bytes 11796484
  99.7 2.1 %copy-start.4 = (f32[96,384]{1,0:T(8,128)}, f32[96,384]{1,0:T(8,128)S(1)}, u32[]{:S(2)}) copy-start(f32[96,384]{1,0:T(8,128)S(1)} %fusion.9) | copy-start | bytes 442372
  102.5 8.4 %all-to-all-start.8 = ((f32[4,1,24]{2,1,0:T(1,128)}), f32[4,1,24]{2,1,0:T(1,128)S(1)}, u32[]{:S(2)}, u32[]{:S(2)}) async-start(f32[4,1,24]{2,1,0:T(1,128)} %bitcast.8), calls=%async_computation.8 | async-start | bytes 4096 | tf_op jit(solution)/shard_map/all_to_all | solution.py:112
  105.7 3.3 %copy-start.2 = (bf16[1,384,5120]{2,1,0:T(8,128)(2,1)S(1)}, bf16[1,384,5120]{2,1,0:T(8,128)(2,1)}, u32[]{:S(2)}) copy-start(bf16[1,384,5120]{2,1,0:T(8,128)(2,1)} %param.12) | copy-start | bytes 11796484
  105.7 3.3 %copy-start.6 = (bf16[96,384]{1,0:T(8,128)(2,1)S(1)}, bf16[96,384]{1,0:T(8,128)(2,1)}, u32[]{:S(2)}) copy-start(bf16[96,384]{1,0:T(8,128)(2,1)} %get-tuple-element.7) | copy-start | bytes 221188
  110.8 18.1 %all-to-all-start.6 = ((bf16[4,24,5120]{2,1,0:T(8,128)(2,1)}), bf16[4,24,5120]{2,1,0:T(8,128)(2,1)}, u32[]{:S(2)}, u32[]{:S(2)}) async-start(bf16[4,24,5120]{2,1,0:T(8,128)(2,1)} %bitcast.50), calls=%async_computation.6 | async-start | bytes 1966080 | tf_op jit(solution)/shard_map/all_to_all | solution.py:103
  128.9 10.0 %all-to-all-start.9 = ((bf16[8,1,3]{2,1,0:T(2,128)(2,1)}), bf16[8,1,3]{2,1,0:T(2,128)(2,1)S(1)}, u32[]{:S(2)}, u32[]{:S(2)}) async-start(bf16[8,1,3]{2,1,0:T(2,128)(2,1)} %convert_element_type.115), calls=%async_computation.9 | async-start | bytes 8192 | tf_op jit(solution)/shard_map/all_to_all | solution.py:123
  138.9 13.2 %all-to-all-start.7 = ((bf16[8,1,3,5120]{3,2,1,0:T(4,128)(2,1)}), bf16[8,1,3,5120]{3,2,1,0:T(4,128)(2,1)}, u32[]{:S(2)}, u32[]{:S(2)}) async-start(bf16[8,1,3,5120]{3,2,1,0:T(4,128)(2,1)} %bitcast.51), calls=%async_computation.7 | async-start | bytes 655360 | tf_op jit(solution)/shard_map/all_to_all | solution.py:122
  143.1 3.1 %copy-start.5 = (f32[96,384]{1,0:T(8,128)S(1)}, f32[96,384]{1,0:T(8,128)}, u32[]{:S(2)}) copy-start(f32[96,384]{1,0:T(8,128)} %copy-done.4) | copy-start | bytes 442372
where the time goes:
time: 156 us; the launch traced here: 155 us
  waiting for transfers between devices  63.4 us (41%)
  starting transfers between devices  39.9 us (26%)
  matrix products  26.9 us (17%)
  local copies, waits for them, and re-layouts  18.6 us (12%)
  other arithmetic  5.14 us (3%)
    all_to_all x1, waiting for transfers between devices, per_device(): lax.all_to_all(spread_dy, 'edp', split_axis=0, concat_axis=0, tiled=True)  13.6 us
    all_to_all x1, waiting for transfers between devices, per_device(): lax.all_to_all(send_x, 'ep', split_axis=0, concat_axis=0, tiled=True)  10.2 us
    all_to_all x1, waiting for transfers between devices, per_device(): lax.all_to_all(spread_x, 'edp', split_axis=0, concat_axis=0, tiled=True)  9.66 us
    all_to_all x1, waiting for transfers between devices, per_device(): lax.all_to_all(partial_half, 'edp', split_axis=0, concat_axis=0, tiled=True)  9.1 us
    all_to_all x1, waiting for transfers between devices, per_device(): lax.all_to_all(send_dy, 'ep', split_axis=0, concat_axis=0, tiled=True)  7.95 us
    all_to_all x1, starting transfers between devices, per_device(): lax.all_to_all(send_p, 'ep', split_axis=0, concat_axis=0, tiled=True)  7.28 us
    all_to_all x1, waiting for transfers between devices, per_device(): lax.all_to_all(send_p, 'ep', split_axis=0, concat_axis=0, tiled=True)  6.36 us
    all_to_all x1, starting transfers between devices, per_device(): lax.all_to_all(slot_dx, 'ep', split_axis=0, concat_axis=0, tiled=True)  4.25 us
  transfers between devices with their start and end apart: 10, of which 9 were waited for; matrix products, arithmetic and copies ran while one was open for 19% of the time, Pallas kernels for 0%

commit v1 on v0

v1 whole, which is shorter than its diff:
```python
import functools

import jax
import jax.numpy as jnp
import numpy as np
from jax import lax
from jax.experimental import pallas as pl
from jax.experimental.pallas import tpu as pltpu
from jax.sharding import PartitionSpec as P

CAP = 3
SUB = 8
LANES = 128
WIDE = SUB * LANES
MESH = pl.DeviceIdType.MESH
F32 = jnp.float32
BF16 = jnp.bfloat16
NT = (((1,), (1,)), ((), ()))
TN = (((0,), (0,)), ((), ()))


def order_matrix(n_ep, per):
    unit = CAP * per
    rows = n_ep * SUB * unit
    out = np.zeros((rows, rows), np.float32)
    for e in range(n_ep):
        for k in range(SUB):
            for kind in range(per):
                for s in range(CAP):
                    out[
                        (e * SUB + k) * unit + kind * CAP + s,
                        ((k * per + kind) * n_ep + e) * CAP + s,
                    ] = 1.0
    return out


def routes(ids, probs, columns):
    tok = ids.shape[0]
    lane = lax.broadcasted_iota(jnp.int32, (tok, LANES), 1)
    expert = lane // CAP
    slot = lane - expert * CAP
    match = jnp.zeros((tok, LANES), F32)
    weight = jnp.zeros((tok, LANES), F32)
    for r in range(ids.shape[1]):
        here = (ids[:, r : r + 1] == expert) & (lane < columns)
        match = jnp.where(here, 1.0, match)
        weight = jnp.where(here, probs[:, r : r + 1].astype(F32), weight)
    row = lax.broadcasted_iota(jnp.int32, (tok, tok), 0)
    col = lax.broadcasted_iota(jnp.int32, (tok, tok), 1)
    earlier = jnp.where(col < row, 1.0, 0.0).astype(BF16)
    before = jnp.dot(earlier, match.astype(BF16), preferred_element_type=F32)
    live = jnp.where(before == slot.astype(F32), match, 0.0)
    return live, live * weight


def main_kernel(
    n_edp, n_ep,
    tok_ref, cot_ref, probs_ref, ids_ref, wg_ref, wu_ref, wd_ref, ord2_ref, ord2t_ref, ord1_ref, ord1t_ref,
    z_out, left_out, back_out, live_out, gp_out,
    w, send_a, recv_a, z, acc, send_b, recv_b, send_c, recv_c, own, send_d, recv_d,
    dp, dp_b, dp_s, dp_c, dp_own, dp_d, dp_r,
    w_sem, z_sem, loc_sem, a_ss, a_rs, e_ss, e_rs, f_ss, f_rs, b_ss, b_rs, c_ss, c_rs, d_ss, d_rs,
    pb_s, pc_ss, pc_rs, pd_ss, pd_rs,
):
    n_ch = z.shape[0]
    hid = wg_ref.shape[1]
    half = n_ep * CAP
    n_q = n_edp // 2
    me_i = lax.axis_index("edp")
    me_j = lax.axis_index("ep")
    q_me = me_i // 2
    core = me_i - q_me * 2
    mate = q_me * 2 + 1 - core

    def w_copy(c, part):
        src = (wg_ref, wu_ref, wd_ref)[part]
        return pltpu.make_async_copy(
            src.at[0, :, pl.ds(pl.multiple_of(c * WIDE, WIDE), WIDE)],
            w.at[c, pl.ds(part * hid, hid), :],
            w_sem.at[c, part],
        )

    barrier = pltpu.get_barrier_semaphore()
    ep_peers = [lax.rem(me_j + o, n_ep) for o in range(1, n_ep)]
    far = [(lax.rem(q_me + o, n_q), o) for o in range(1, n_q)]
    for j in ep_peers:
        pl.semaphore_signal(barrier, inc=1, device_id=(me_i, j), device_id_type=MESH)
    for q, _ in far:
        pl.semaphore_signal(barrier, inc=1, device_id=(q * 2 + core, me_j), device_id_type=MESH)
    pl.semaphore_signal(barrier, inc=1, device_id=(mate, me_j), device_id_type=MESH)

    live, scaled = routes(ids_ref[...], probs_ref[...], half)
    live_out[...] = live.astype(BF16)
    live_t = live.T[:half].astype(BF16)
    scaled_t = scaled.T[:half].astype(BF16)
    prob = jnp.sum(scaled, axis=0, keepdims=True)

    pl.semaphore_wait(barrier, n_ep - 1 + n_q - 1 + 1)

    def remote(src, dst, ss, rs, i, j):
        return pltpu.make_async_remote_copy(
            src_ref=src, dst_ref=dst, send_sem=ss, recv_sem=rs, device_id=(i, j), device_id_type=MESH
        )

    def a_copy(c, j, slot):
        return remote(send_a.at[c, j], recv_a.at[c, slot], a_ss.at[c, j], a_rs.at[c, slot], me_i, j)

    def a_own(c):
        return pltpu.make_async_copy(send_a.at[c, me_j], recv_a.at[c, me_j], loc_sem.at[c])

    def pack(c, _):
        cols = pl.ds(pl.multiple_of(c * WIDE, WIDE), WIDE)
        x = jnp.dot(live_t, tok_ref[:, cols], preferred_element_type=F32)
        y = jnp.dot(scaled_t, cot_ref[:, cols], preferred_element_type=F32)
        parts = []
        for k in range(SUB):
            lanes = slice(k * LANES, (k + 1) * LANES)
            parts += [x[:, lanes], y[:, lanes]]
        mixed = jnp.concatenate(parts, axis=0).astype(BF16)
        packed = jnp.dot(ord2_ref[...], mixed, preferred_element_type=F32)
        send_a[c] = packed.astype(BF16).reshape(send_a.shape[1:])
        for j in ep_peers:
            a_copy(c, j, me_j).start()
        a_own(c).start()
        for part in range(3):
            w_copy(c, part).start()
        return 0

    lax.fori_loop(0, n_ch, pack, 0)

    def e_copy(c, i, slot, o):
        return remote(z.at[c, me_i], z.at[c, slot], e_ss.at[c, o], e_rs.at[c, o], i, me_j)

    def f_copy(c, slot, o):
        return remote(z.at[c, slot], z.at[c, slot], f_ss.at[c, o], f_rs.at[c, o], mate, me_j)

    def gather(t, _):
        @pl.when(t < n_ch)
        def _():
            c = t
            for j in ep_peers:
                a_copy(c, j, j).wait_recv()
            a_own(c).wait()
            mixed = recv_a[c].reshape(ord2_ref.shape[0], LANES)
            rows = jnp.dot(ord2t_ref[...], mixed, preferred_element_type=F32)
            wide = jnp.concatenate(
                [rows[k * 2 * half : (k + 1) * 2 * half] for k in range(SUB)], axis=1
            )
            z[c, me_i] = wide.astype(BF16)
            for q, o in far:
                e_copy(c, q * 2 + core, me_i, o).start()
            e_copy(c, mate, me_i, 0).start()

        @pl.when((t >= 1) & (t < n_ch + 1))
        def _():
            c = t - 1
            for _, o in far:
                from_q = lax.rem(q_me - o + n_q, n_q)
                e_copy(c, from_q * 2 + core, from_q * 2 + core, o).wait_recv()
                f_copy(c, from_q * 2 + core, o).start()

        @pl.when(t >= 2)
        def _():
            c = t - 2
            e_copy(c, mate, mate, 0).wait_recv()
            for _, o in far:
                from_q = lax.rem(q_me - o + n_q, n_q)
                f_copy(c, from_q * 2 + 1 - core, o).wait_recv()
            for part in range(3):
                w_copy(c, part).wait()
            rows = z[c].reshape(n_edp * 2 * half, WIDE)
            part = lax.dot_general(rows, w[c], NT, preferred_element_type=F32)

            @pl.when(c == 0)
            def _():
                acc[...] = part

            @pl.when(c > 0)
            def _():
                acc[...] += part

        return 0

    lax.fori_loop(0, n_ch + 2, gather, 0)

    def z_copy(c):
        return pltpu.make_async_copy(z.at[c], z_out.at[c], z_sem.at[c])

    def z_start(c, _):
        z_copy(c).start()
        return 0

    lax.fori_loop(0, n_ch, z_start, 0)

    both = []
    left = []
    none = jnp.zeros((half, hid), F32)
    for i in range(n_edp):
        first = i * 2 * half
        a = acc[first : first + half, :hid]
        u = acc[first : first + half, hid : 2 * hid]
        g = acc[first + half : first + 2 * half, 2 * hid :]
        s = jax.nn.sigmoid(a)
        h = a * s * u
        d_a = g * u * s * (1.0 + a * (1.0 - s))
        d_u = g * a * s
        both.append(jnp.concatenate([d_a, d_u], axis=1))
        left.append(jnp.concatenate([d_a, d_u, none], axis=1))
        left.append(jnp.concatenate([none, none, h], axis=1))
        dp[i] = jnp.broadcast_to(jnp.sum(h * g, axis=1, keepdims=True), (half, LANES))
    both = jnp.concatenate(both, axis=0).astype(BF16)
    left_out[...] = jnp.concatenate(left, axis=0).astype(BF16)

    def b_copy(c, q):
        return remote(
            send_b.at[c, q * 2 + 1 - core], recv_b.at[c, q], b_ss.at[c, q], b_rs.at[c, q], mate, me_j
        )

    def dpb_copy(q):
        return remote(dp.at[q * 2 + 1 - core], dp_b.at[q], pb_s.at[0, q], pb_s.at[1, q], mate, me_j)

    def c_copy(c, q, o):
        return remote(
            send_c.at[c, o - 1], recv_c.at[c, o - 1], c_ss.at[c, o - 1], c_rs.at[c, o - 1], q * 2 + core, me_j
        )

    def dpc_copy(q, o):
        return remote(
            dp_s.at[o - 1], dp_c.at[o - 1], pc_ss.at[o - 1], pc_rs.at[o - 1], q * 2 + core, me_j
        )

    def d_copy(c, j, slot):
        return remote(send_d.at[c, j], recv_d.at[c, slot], d_ss.at[c, j], d_rs.at[c, slot], me_i, j)

    def dpd_copy(j, slot):
        return remote(dp_d, dp_r.at[slot], pd_ss.at[j], pd_rs.at[slot], me_i, j)

    for q in range(n_q):
        dpb_copy(q).start()

    def give_back(t, _):
        @pl.when(t < n_ch)
        def _():
            c = t
            part = jnp.dot(both, w[c, : 2 * hid, :], preferred_element_type=F32)
            for i in range(n_edp):
                send_b[c, i] = part[i * half : (i + 1) * half].astype(BF16)
            for q in range(n_q):
                b_copy(c, q).start()

        @pl.when((t >= 1) & (t < n_ch + 1))
        def _():
            c = t - 1
            for q in range(n_q):
                b_copy(c, q).wait_recv()
            for q, o in far:
                total = send_b[c, q * 2 + core].astype(F32) + recv_b[c, q].astype(F32)
                send_c[c, o - 1] = total.astype(BF16)
                c_copy(c, q, o).start()
            own[c] = send_b[c, me_i].astype(F32) + recv_b[c, q_me].astype(F32)

        @pl.when(t >= 2)
        def _():
            c = t - 2
            total = own[c]
            for q, o in far:
                c_copy(c, q, o).wait_recv()
                total = total + recv_c[c, o - 1].astype(F32)
            mixed = jnp.concatenate(
                [total[:, k * LANES : (k + 1) * LANES] for k in range(SUB)], axis=0
            ).astype(BF16)
            packed = jnp.dot(ord1_ref[...], mixed, preferred_element_type=F32)
            send_d[c] = packed.astype(BF16).reshape(send_d.shape[1:])
            for j in ep_peers:
                d_copy(c, j, me_j).start()
            recv_d[c, me_j] = send_d[c, me_j]

        return 0

    lax.fori_loop(0, n_ch + 2, give_back, 0)

    for q in range(n_q):
        dpb_copy(q).wait_recv()
    for q, o in far:
        dp_s[o - 1] = dp[q * 2 + core] + dp_b[q]
        dpc_copy(q, o).start()
    total = dp[me_i] + dp_b[q_me]
    for q, o in far:
        dpc_copy(q, o).wait_recv()
        total = total + dp_c[o - 1]
    square = jnp.concatenate([total, jnp.zeros((LANES - half, LANES), F32)], axis=0)
    dp_d[...] = square.T[:1]
    for j in ep_peers:
        dpd_copy(j, me_j).start()
    dp_r[me_j] = dp_d[...]

    def finish(c, _):
        for j in ep_peers:
            d_copy(c, j, j).wait_recv()
        mixed = recv_d[c].reshape(ord1_ref.shape[0], LANES)
        rows = jnp.dot(ord1t_ref[...], mixed, preferred_element_type=F32)
        wide = jnp.concatenate([rows[k * half : (k + 1) * half] for k in range(SUB)], axis=1)
        back_out[c] = wide.astype(BF16)
        return 0

    lax.fori_loop(0, n_ch, finish, 0)

    for j in ep_peers:
        dpd_copy(j, j).wait_recv()
    lane = lax.broadcasted_iota(jnp.int32, (1, LANES), 1)
    got = jnp.zeros((1, LANES), F32)
    for e in range(n_ep):
        for s in range(CAP):
            value = jnp.sum(
                jnp.where(lane == me_j * CAP + s, dp_r[e], 0.0), axis=1, keepdims=True
            )
            got = jnp.where(lane == e * CAP + s, value, got)
    gp_out[...] = jnp.where(prob > 0.0, got / jnp.where(prob > 0.0, prob, 1.0), 0.0)

    def drain(c, _):
        for j in ep_peers:
            a_copy(c, j, me_j).wait_send()
            d_copy(c, j, me_j).wait_send()
        e_copy(c, mate, me_i, 0).wait_send()
        for q, o in far:
            e_copy(c, q * 2 + core, me_i, o).wait_send()
            f_copy(c, q * 2 + core, o).wait_send()
            c_copy(c, q, o).wait_send()
        for q in range(n_q):
            b_copy(c, q).wait_send()
        z_copy(c).wait()
        return 0

    lax.fori_loop(0, n_ch, drain, 0)
    for q in range(n_q):
        dpb_copy(q).wait_send()
    for q, o in far:
        dpc_copy(q, o).wait_send()
    for j in ep_peers:
        dpd_copy(j, me_j).wait_send()


def exchange(n_edp, n_ep, tokens, cotangent, gate_probs, expert_ids, w_gate, w_up, w_down):
    tok, width = tokens.shape
    hid = w_gate.shape[1]
    half = n_ep * CAP
    n_q = n_edp // 2
    n_far = max(n_q - 1, 1)
    n_ch = width // WIDE
    two = order_matrix(n_ep, 2)
    one = order_matrix(n_ep, 1)
    orders = [jnp.asarray(m, BF16) for m in (two, two.T, one, one.T)]
    vmem = pl.BlockSpec(memory_space=pltpu.VMEM)
    hbm = pl.BlockSpec(memory_space=pl.ANY)
    dma = pltpu.SemaphoreType.DMA
    rows = n_edp * 2 * half
    return pl.pallas_call(
        functools.partial(main_kernel, n_edp, n_ep),
        out_shape=(
            jax.ShapeDtypeStruct((n_ch, n_edp, 2 * half, WIDE), BF16),
            jax.ShapeDtypeStruct((rows, 3 * hid), BF16),
            jax.ShapeDtypeStruct((n_ch, half, WIDE), BF16),
            jax.ShapeDtypeStruct((tok, LANES), BF16),
            jax.ShapeDtypeStruct((1, LANES), F32),
        ),
        in_specs=[vmem] * 4 + [hbm] * 3 + [vmem] * 4,
        out_specs=(hbm, vmem, vmem, vmem, vmem),
        scratch_shapes=[
            pltpu.VMEM((n_ch, 3 * hid, WIDE), BF16),
            pltpu.VMEM((n_ch, n_ep, SUB * 2 * CAP, LANES), BF16),
            pltpu.VMEM((n_ch, n_ep, SUB * 2 * CAP, LANES), BF16),
            pltpu.VMEM((n_ch, n_edp, 2 * half, WIDE), BF16),
            pltpu.VMEM((rows, 3 * hid), F32),
            pltpu.VMEM((n_ch, n_edp, half, WIDE), BF16),
            pltpu.VMEM((n_ch, n_q, half, WIDE), BF16),
            pltpu.VMEM((n_ch, n_far, half, WIDE), BF16),
            pltpu.VMEM((n_ch, n_far, half, WIDE), BF16),
            pltpu.VMEM((n_ch, half, WIDE), F32),
            pltpu.VMEM((n_ch, n_ep, SUB * CAP, LANES), BF16),
            pltpu.VMEM((n_ch, n_ep, SUB * CAP, LANES), BF16),
            pltpu.VMEM((n_edp, half, LANES), F32),
            pltpu.VMEM((n_q, half, LANES), F32),
            pltpu.VMEM((n_far, half, LANES), F32),
            pltpu.VMEM((n_far, half, LANES), F32),
            pltpu.VMEM((half, LANES), F32),
            pltpu.VMEM((1, LANES), F32),
            pltpu.VMEM((n_ep, 1, LANES), F32),
            dma((n_ch, 3)),
            dma((n_ch,)),
            dma((n_ch,)),
            dma((n_ch, n_ep)),
            dma((n_ch, n_ep)),
            dma((n_ch, n_q)),
            dma((n_ch, n_q)),
            dma((n_ch, n_q)),
            dma((n_ch, n_q)),
            dma((n_ch, n_q)),
            dma((n_ch, n_q)),
            dma((n_ch, n_far)),
            dma((n_ch, n_far)),
            dma((n_ch, n_ep)),
            dma((n_ch, n_ep)),
            dma((2, n_q)),
            dma((n_far,)),
            dma((n_far,)),
            dma((n_ep,)),
            dma((n_ep,)),
        ],
        compiler_params=pltpu.CompilerParams(
            collective_id=0, has_side_effects=True, vmem_limit_bytes=60 * 2**20
        ),
    )(tokens, cotangent, gate_probs, expert_ids, w_gate, w_up, w_down, *orders)


def grads_kernel(half, z_ref, left_ref, back_ref, live_ref, gp_ref, ids_ref, tg_ref, gg_ref, wg_ref, wu_ref, wd_ref):
    hid = wg_ref.shape[1]
    rows = z_ref[0].reshape(left_ref.shape[0], WIDE)
    for part, out in enumerate((wg_ref, wu_ref, wd_ref)):
        out[0] = lax.dot_general(
            left_ref[:, part * hid : (part + 1) * hid], rows, TN, preferred_element_type=F32
        ).astype(BF16)
    live = live_ref[...]
    tg_ref[...] = jnp.dot(live[:, :half], back_ref[0], preferred_element_type=F32).astype(BF16)

    @pl.when(pl.program_id(0) == 0)
    def _():
        ids = ids_ref[...]
        expert = lax.broadcasted_iota(jnp.int32, live.shape, 1) // CAP
        value = live.astype(F32) * gp_ref[...]
        for r in range(ids.shape[1]):
            mine = jnp.where(ids[:, r : r + 1] == expert, value, 0.0)
            gg_ref[:, r : r + 1] = jnp.sum(mine, axis=1, keepdims=True).astype(BF16)


def per_device(tokens, cotangent, gate_probs, expert_ids, w_gate, w_up, w_down):
    n_edp = lax.axis_size("edp")
    n_ep = lax.axis_size("ep")
    half = n_ep * CAP
    z, left, back, live, gp = exchange(
        n_edp, n_ep, tokens, cotangent, gate_probs, expert_ids, w_gate, w_up, w_down
    )
    n_ch = z.shape[0]
    tok, width = tokens.shape
    hid = w_gate.shape[1]
    rows = left.shape[0]

    def whole(shape):
        return pl.BlockSpec(shape, lambda c: (0,) * len(shape))

    w_spec = pl.BlockSpec((1, hid, WIDE), lambda c: (0, 0, c))
    w_shape = jax.ShapeDtypeStruct(w_gate.shape, BF16)
    return pl.pallas_call(
        functools.partial(grads_kernel, half),
        grid=(n_ch,),
        out_shape=(
            jax.ShapeDtypeStruct((tok, width), BF16),
            jax.ShapeDtypeStruct(gate_probs.shape, BF16),
            w_shape,
            w_shape,
            w_shape,
        ),
        in_specs=[
            pl.BlockSpec((1, n_edp, 2 * half, WIDE), lambda c: (c, 0, 0, 0)),
            whole((rows, 3 * hid)),
            pl.BlockSpec((1, half, WIDE), lambda c: (c, 0, 0)),
            whole((tok, LANES)),
            whole((1, LANES)),
            whole(expert_ids.shape),
        ],
        out_specs=(
            pl.BlockSpec((tok, WIDE), lambda c: (0, c)),
            whole(gate_probs.shape),
            w_spec,
            w_spec,
            w_spec,
        ),
        compiler_params=pltpu.CompilerParams(vmem_limit_bytes=48 * 2**20),
    )(z, left, back, live, gp, expert_ids)


def solution(mesh):
    rows = P(("edp", "ep"), None)
    weights = P("ep", "edp", None)
    return jax.shard_map(
        per_device,
        mesh=mesh,
        in_specs=(rows, rows, rows, rows, weights, weights, weights),
        out_specs=(rows, rows, weights, weights, weights),
        check_vma=False,
    )
```

time: 156 us -> 70.6 us (0.45)
  waiting for transfers between devices: 63.4 us -> 0 us
  Pallas kernels: 0 us -> 61.2 us
  starting transfers between devices: 39.9 us -> 0 us
  matrix products: 26.9 us -> 0 us
  local copies, waits for them, and re-layouts: 18.6 us -> 8.39 us
  other arithmetic: 5.14 us -> 0 us
    all_to_all x10 -> x0, waiting for transfers between devices: 63.4 us -> none  [the longest x1 13.6 us: per_device(): lax.all_to_all(spread_dy, 'edp', split_axis=0, concat_axis=0, tiled=True)]
    pallas_call x0 -> x2, Pallas kernels: none -> 61.2 us  [the longest x1 53.6 us: exchange(): pl.pallas_call(functools.partial(main_kernel, n_edp, n_ep), out_shape=(ja...]
    all_to_all x10 -> x0, starting transfers between devices: 39.9 us -> none  [the longest x1 7.28 us: per_device(): lax.all_to_all(send_p, 'ep', split_axis=0, concat_axis=0, tiled=True)]
    dot_general x14 -> x0, matrix products: 26.9 us -> none  [the longest x1 4.02 us: per_device(): lax.dot_general(grad_up, x_rows, outer, preferred_element_type=jnp.float32)]
    reshape x9 -> x0, local copies, waits for them, and re-layouts: 9.57 us -> none  [the longest x3 2.66 us: spread_rows(): return jnp.repeat(grouped.transpose(order), split, axis=0)]
    unnamed x14, local copies, waits for them, and re-layouts: 0.18 us -> 7.72 us
    all_to_all x7 -> x0, local copies, waits for them, and re-layouts: 5.45 us -> none  [the longest x1 1.91 us: per_device(): lax.all_to_all(spread_dy, 'edp', split_axis=0, concat_axis=0, tiled=True)]
    reduce_sum x5 -> x0, other arithmetic: 3.73 us -> none  [the longest x1 2.11 us: per_device(): jnp.sum(came_dx.reshape(EXP_EP, split, ep_size * capacity, model_width).a...]
  transfers between devices with their start and end apart: 10 -> 0, of which waited for: 9 -> 0; matrix products, arithmetic and copies ran while one was open for 19% -> 0% of each run, Pallas kernels for 0% -> 0%
where the time goes in v1:
time: 70.6 us; the launch traced here: 70.2 us
  Pallas kernels  61.2 us (87%)
  local copies, waits for them, and re-layouts  8.39 us (12%)
    pallas_call x1, Pallas kernels, exchange(): pl.pallas_call(functools.partial(main_kernel, n_edp, n_ep), out_shape=(ja...  53.6 us
    unnamed x14, local copies, waits for them, and re-layouts  7.72 us
    pallas_call x1, Pallas kernels, per_device(): pl.pallas_call(functools.partial(grads_kernel, half), grid=(n_ch,), out_s...  7.59 us

profile of v1, /device:TPU:0, one launch (start us, length us, event | category | flops | bytes accessed | tf_op | source)
XLA Modules:
  0.0 70.2 jit_solution(14802177107283526587)
XLA Ops:
  0.6 1.4 %copy.16.probs_ref = bf16[128,6]{1,0:T(8,128)(2,1)} copy(bf16[128,6]{0,1:T(8,128)(2,1)} %param.13) | data formatting | bytes 3072 | tf_op args[2]
  2.0 1.4 %copy.17.ids_ref = s32[128,6]{1,0:T(8,128)} copy(s32[128,6]{0,1:T(8,128)} %param.14) | data formatting | bytes 6144 | tf_op args[3]
  3.5 0.0 copy-start.1
  3.5 53.6 %shard_map.146 = (bf16[5,4,48,1024]{3,2,1,0:T(8,128)(2,1)}, bf16[192,1152]{1,0:T(8,128)(2,1)}, bf16[5,24,1024]{2,1,0:T(8,128)(2,1)}, bf16[128,128]{1,0:T(8,128)(2,1)}, f32[1,128]{1,0:T(1,128)}) custom-call(bf16[128,5120]{1,0:T(8,128)(2,1)} %tok_ref.1, bf16[128,5120]{1,0:T(8,128)(2,1)} %cot_ref.1, bf16[128,6]{1,0:T(8,128)(2,1)} %copy.16.probs_ref, ...), custom_call_target="tpu_custom_call" | custom-call | tf_op jit(solution)/shard_map/pallas_call | solution.py:357
  57.1 0.0 copy-done.1
  57.1 0.0 copy-start
  57.1 1.5 %copy-done = bf16[5,4,48,1024]{3,2,1,0:T(8,128)(2,1)S(1)} copy-done((bf16[5,4,48,1024]{3,2,1,0:T(8,128)(2,1)S(1)}, bf16[5,4,48,1024]{3,2,1,0:T(8,128)(2,1)}, u32[]{:S(2)}) %copy-start) | copy-done | bytes 1966104
  58.6 0.0 copy-start.2
  58.6 1.0 %copy-done.2 = bf16[192,1152]{1,0:T(8,128)(2,1)S(1)} copy-done((bf16[192,1152]{1,0:T(8,128)(2,1)S(1)}, bf16[192,1152]{1,0:T(8,128)(2,1)}, u32[]{:S(2)}) %copy-start.2) | copy-done | bytes 442392
  59.6 0.0 copy-start.3
  59.6 0.9 %copy-done.3 = bf16[5,24,1024]{2,1,0:T(8,128)(2,1)S(1)} copy-done((bf16[5,24,1024]{2,1,0:T(8,128)(2,1)S(1)}, bf16[5,24,1024]{2,1,0:T(8,128)(2,1)}, u32[]{:S(2)}) %copy-start.3) | copy-done | bytes 245784
  60.6 0.0 copy-start.4
  60.6 0.8 %copy-done.4 = bf16[128,128]{1,0:T(8,128)(2,1)S(1)} copy-done((bf16[128,128]{1,0:T(8,128)(2,1)S(1)}, bf16[128,128]{1,0:T(8,128)(2,1)}, u32[]{:S(2)}) %copy-start.4) | copy-done | bytes 32792
  61.3 0.0 copy-start.5
  61.4 0.6 copy-done.5
  62.0 7.6 %shard_map.147 = (bf16[128,5120]{1,0:T(8,128)(2,1)}, bf16[128,6]{1,0:T(8,128)(2,1)S(1)}, bf16[1,384,5120]{2,1,0:T(8,128)(2,1)}, bf16[1,384,5120]{2,1,0:T(8,128)(2,1)}, bf16[1,384,5120]{2,1,0:T(8,128)(2,1)}) custom-call(bf16[5,4,48,1024]{3,2,1,0:T(8,128)(2,1)S(1)} %copy-done, bf16[192,1152]{1,0:T(8,128)(2,1)S(1)} %copy-done.2, ...), custom_call_target="tpu_custom_call" | custom-call | tf_op jit(solution)/shard_map/pallas_call | solution.py:452
  69.6 0.7 copy.19
Async XLA Ops:
  3.5 53.6 %copy-start.1 = (s32[128,6]{1,0:T(8,128)S(1)}, s32[128,6]{1,0:T(8,128)}, u32[]{:S(2)}) copy-start(s32[128,6]{1,0:T(8,128)} %copy.17.ids_ref) | copy-start | bytes 9220
  57.1 1.5 %copy-start = (bf16[5,4,48,1024]{3,2,1,0:T(8,128)(2,1)S(1)}, bf16[5,4,48,1024]{3,2,1,0:T(8,128)(2,1)}, u32[]{:S(2)}) copy-start(bf16[5,4,48,1024]{3,2,1,0:T(8,128)(2,1)} %get-tuple-element.10.z_ref) | copy-start | bytes 5898244
  58.6 1.0 %copy-start.2 = (bf16[192,1152]{1,0:T(8,128)(2,1)S(1)}, bf16[192,1152]{1,0:T(8,128)(2,1)}, u32[]{:S(2)}) copy-start(bf16[192,1152]{1,0:T(8,128)(2,1)} %get-tuple-element.11.left_ref) | copy-start | bytes 1327108
  59.6 0.9 %copy-start.3 = (bf16[5,24,1024]{2,1,0:T(8,128)(2,1)S(1)}, bf16[5,24,1024]{2,1,0:T(8,128)(2,1)}, u32[]{:S(2)}) copy-start(bf16[5,24,1024]{2,1,0:T(8,128)(2,1)} %get-tuple-element.12.back_ref) | copy-start | bytes 737284
  60.6 0.8 %copy-start.4 = (bf16[128,128]{1,0:T(8,128)(2,1)S(1)}, bf16[128,128]{1,0:T(8,128)(2,1)}, u32[]{:S(2)}) copy-start(bf16[128,128]{1,0:T(8,128)(2,1)} %get-tuple-element.13.live_ref) | copy-start | bytes 98308
  61.3 0.6 copy-start.5

commit v2 on v1

--- a/solution.py
+++ b/solution.py
@@ -35,20 +35,20 @@
 
 
 def routes(ids, probs, columns):
-    tok = ids.shape[0]
-    lane = lax.broadcasted_iota(jnp.int32, (tok, LANES), 1)
-    expert = lane // CAP
-    slot = lane - expert * CAP
-    match = jnp.zeros((tok, LANES), F32)
-    weight = jnp.zeros((tok, LANES), F32)
-    for r in range(ids.shape[1]):
-        here = (ids[:, r : r + 1] == expert) & (lane < columns)
+    tok = ids.shape[1]
+    row = lax.broadcasted_iota(jnp.int32, (columns, tok), 0)
+    expert = row // CAP
+    slot = row - expert * CAP
+    match = jnp.zeros((columns, tok), F32)
+    weight = jnp.zeros((columns, tok), F32)
+    for r in range(ids.shape[0]):
+        here = ids[r : r + 1] == expert
         match = jnp.where(here, 1.0, match)
-        weight = jnp.where(here, probs[:, r : r + 1].astype(F32), weight)
-    row = lax.broadcasted_iota(jnp.int32, (tok, tok), 0)
-    col = lax.broadcasted_iota(jnp.int32, (tok, tok), 1)
-    earlier = jnp.where(col < row, 1.0, 0.0).astype(BF16)
-    before = jnp.dot(earlier, match.astype(BF16), preferred_element_type=F32)
+        weight = jnp.where(here, probs[r : r + 1], weight)
+    first = lax.broadcasted_iota(jnp.int32, (tok, tok), 0)
+    second = lax.broadcasted_iota(jnp.int32, (tok, tok), 1)
+    earlier = jnp.where(first < second, 1.0, 0.0).astype(BF16)
+    before = jnp.dot(match.astype(BF16), earlier, preferred_element_type=F32)
     live = jnp.where(before == slot.astype(F32), match, 0.0)
     return live, live * weight
 
@@ -57,9 +57,9 @@
     n_edp, n_ep,
     tok_ref, cot_ref, probs_ref, ids_ref, wg_ref, wu_ref, wd_ref, ord2_ref, ord2t_ref, ord1_ref, ord1t_ref,
     z_out, left_out, back_out, live_out, gp_out,
-    w, send_a, recv_a, z, acc, send_b, recv_b, send_c, recv_c, own, send_d, recv_d,
-    dp, dp_b, dp_s, dp_c, dp_own, dp_d, dp_r,
-    w_sem, z_sem, loc_sem, a_ss, a_rs, e_ss, e_rs, f_ss, f_rs, b_ss, b_rs, c_ss, c_rs, d_ss, d_rs,
+    tok, cot, w, send_a, recv_a, z, acc, send_b, recv_b, send_c, recv_c, own, send_d, recv_d,
+    dp, dp_b, dp_s, dp_c, dp_d, dp_r,
+    t_sem, w_sem, z_sem, loc_sem, a_ss, a_rs, e_ss, e_rs, f_ss, f_rs, b_ss, b_rs, c_ss, c_rs, d_ss, d_rs,
     pb_s, pc_ss, pc_rs, pd_ss, pd_rs,
 ):
     n_ch = z.shape[0]
@@ -80,6 +80,16 @@
             w_sem.at[c, part],
         )
 
+    def t_copy(c, part):
+        src, dst = ((tok_ref, tok), (cot_ref, cot))[part]
+        return pltpu.make_async_copy(
+            src.at[:, pl.ds(pl.multiple_of(c * WIDE, WIDE), WIDE)], dst.at[c], t_sem.at[c, part]
+        )
+
+    for c in range(n_ch):
+        t_copy(c, 0).start()
+        t_copy(c, 1).start()
+
     barrier = pltpu.get_barrier_semaphore()
     ep_peers = [lax.rem(me_j + o, n_ep) for o in range(1, n_ep)]
     far = [(lax.rem(q_me + o, n_q), o) for o in range(1, n_q)]
@@ -91,9 +101,9 @@
 
     live, scaled = routes(ids_ref[...], probs_ref[...], half)
     live_out[...] = live.astype(BF16)
-    live_t = live.T[:half].astype(BF16)
-    scaled_t = scaled.T[:half].astype(BF16)
-    prob = jnp.sum(scaled, axis=0, keepdims=True)
+    live_t = live.astype(BF16)
+    scaled_t = scaled.astype(BF16)
+    prob = jnp.sum(scaled, axis=1, keepdims=True)
 
     pl.semaphore_wait(barrier, n_ep - 1 + n_q - 1 + 1)
 
@@ -109,9 +119,10 @@
         return pltpu.make_async_copy(send_a.at[c, me_j], recv_a.at[c, me_j], loc_sem.at[c])
 
     def pack(c, _):
-        cols = pl.ds(pl.multiple_of(c * WIDE, WIDE), WIDE)
-        x = jnp.dot(live_t, tok_ref[:, cols], preferred_element_type=F32)
-        y = jnp.dot(scaled_t, cot_ref[:, cols], preferred_element_type=F32)
+        t_copy(c, 0).wait()
+        t_copy(c, 1).wait()
+        x = jnp.dot(live_t, tok[c], preferred_element_type=F32)
+        y = jnp.dot(scaled_t, cot[c], preferred_element_type=F32)
         parts = []
         for k in range(SUB):
             lanes = slice(k * LANES, (k + 1) * LANES)
@@ -169,7 +180,7 @@
             for part in range(3):
                 w_copy(c, part).wait()
             rows = z[c].reshape(n_edp * 2 * half, WIDE)
-            part = lax.dot_general(rows, w[c], NT, preferred_element_type=F32)
+            part = lax.dot_general(w[c], rows, NT, preferred_element_type=F32)
 
             @pl.when(c == 0)
             def _():
@@ -192,32 +203,29 @@
 
     lax.fori_loop(0, n_ch, z_start, 0)
 
-    both = []
-    left = []
-    none = jnp.zeros((half, hid), F32)
-    for i in range(n_edp):
-        first = i * 2 * half
-        a = acc[first : first + half, :hid]
-        u = acc[first : first + half, hid : 2 * hid]
-        g = acc[first + half : first + 2 * half, 2 * hid :]
-        s = jax.nn.sigmoid(a)
-        h = a * s * u
-        d_a = g * u * s * (1.0 + a * (1.0 - s))
-        d_u = g * a * s
-        both.append(jnp.concatenate([d_a, d_u], axis=1))
-        left.append(jnp.concatenate([d_a, d_u, none], axis=1))
-        left.append(jnp.concatenate([none, none, h], axis=1))
-        dp[i] = jnp.broadcast_to(jnp.sum(h * g, axis=1, keepdims=True), (half, LANES))
-    both = jnp.concatenate(both, axis=0).astype(BF16)
-    left_out[...] = jnp.concatenate(left, axis=0).astype(BF16)
+    n_rows = n_edp * 2 * half
+    a = acc[:hid]
+    u = acc[hid : 2 * hid]
+    g = pltpu.roll(acc[2 * hid :], n_rows - half, 1)
+    lane = lax.broadcasted_iota(jnp.int32, (hid, n_rows), 1)
+    is_x = lax.rem(lane // half, 2) == 0
+    s = jax.nn.sigmoid(a)
+    h = a * s * u
+    d_a = jnp.where(is_x, g * u * s * (1.0 + a * (1.0 - s)), 0.0)
+    d_u = jnp.where(is_x, g * a * s, 0.0)
+    acc[:hid] = d_a
+    acc[hid : 2 * hid] = d_u
+    acc[2 * hid :] = jnp.where(is_x, h, 0.0)
+    dp[...] = jnp.sum(jnp.where(is_x, h * g, 0.0), axis=0, keepdims=True)
+    both = acc[: 2 * hid].T.astype(BF16)
 
     def b_copy(c, q):
         return remote(
             send_b.at[c, q * 2 + 1 - core], recv_b.at[c, q], b_ss.at[c, q], b_rs.at[c, q], mate, me_j
         )
 
-    def dpb_copy(q):
-        return remote(dp.at[q * 2 + 1 - core], dp_b.at[q], pb_s.at[0, q], pb_s.at[1, q], mate, me_j)
+    def dpb_copy():
+        return remote(dp, dp_b, pb_s.at[0], pb_s.at[1], mate, me_j)
 
     def c_copy(c, q, o):
         return remote(
@@ -225,9 +233,7 @@
         )
 
     def dpc_copy(q, o):
-        return remote(
-            dp_s.at[o - 1], dp_c.at[o - 1], pc_ss.at[o - 1], pc_rs.at[o - 1], q * 2 + core, me_j
-        )
+        return remote(dp_s, dp_c.at[o - 1], pc_ss.at[o - 1], pc_rs.at[o - 1], q * 2 + core, me_j)
 
     def d_copy(c, j, slot):
         return remote(send_d.at[c, j], recv_d.at[c, slot], d_ss.at[c, j], d_rs.at[c, slot], me_i, j)
@@ -235,8 +241,7 @@
     def dpd_copy(j, slot):
         return remote(dp_d, dp_r.at[slot], pd_ss.at[j], pd_rs.at[slot], me_i, j)
 
-    for q in range(n_q):
-        dpb_copy(q).start()
+    dpb_copy().start()
 
     def give_back(t, _):
         @pl.when(t < n_ch)
@@ -244,7 +249,7 @@
             c = t
             part = jnp.dot(both, w[c, : 2 * hid, :], preferred_element_type=F32)
             for i in range(n_edp):
-                send_b[c, i] = part[i * half : (i + 1) * half].astype(BF16)
+                send_b[c, i] = part[i * 2 * half : (i * 2 + 1) * half].astype(BF16)
             for q in range(n_q):
                 b_copy(c, q).start()
 
@@ -258,6 +263,13 @@
                 send_c[c, o - 1] = total.astype(BF16)
                 c_copy(c, q, o).start()
             own[c] = send_b[c, me_i].astype(F32) + recv_b[c, q_me].astype(F32)
+
+            @pl.when(c == 0)
+            def _():
+                dpb_copy().wait_recv()
+                dp_s[...] = dp[...] + dp_b[...]
+                for q, o in far:
+                    dpc_copy(q, o).start()
 
         @pl.when(t >= 2)
         def _():
@@ -275,24 +287,24 @@
                 d_copy(c, j, me_j).start()
             recv_d[c, me_j] = send_d[c, me_j]
 
+            @pl.when(c == 0)
+            def _():
+                whole_dp = dp_s[...]
+                for q, o in far:
+                    dpc_copy(q, o).wait_recv()
+                    whole_dp = whole_dp + dp_c[o - 1]
+                dp_d[...] = whole_dp
+                dp_r[me_j] = whole_dp
+                for j in ep_peers:
+                    dpd_copy(j, me_j).start()
+
         return 0
 
     lax.fori_loop(0, n_ch + 2, give_back, 0)
 
-    for q in range(n_q):
-        dpb_copy(q).wait_recv()
-    for q, o in far:
-        dp_s[o - 1] = dp[q * 2 + core] + dp_b[q]
-        dpc_copy(q, o).start()
-    total = dp[me_i] + dp_b[q_me]
-    for q, o in far:
-        dpc_copy(q, o).wait_recv()
-        total = total + dp_c[o - 1]
-    square = jnp.concatenate([total, jnp.zeros((LANES - half, LANES), F32)], axis=0)
-    dp_d[...] = square.T[:1]
-    for j in ep_peers:
-        dpd_copy(j, me_j).start()
-    dp_r[me_j] = dp_d[...]
+    spin = pltpu.roll(acc[2 * hid :], half, 1)
+    left_out[: 2 * hid] = acc[: 2 * hid].astype(BF16)
+    left_out[2 * hid :] = spin.astype(BF16)
 
     def finish(c, _):
         for j in ep_peers:
@@ -307,15 +319,15 @@
 
     for j in ep_peers:
         dpd_copy(j, j).wait_recv()
-    lane = lax.broadcasted_iota(jnp.int32, (1, LANES), 1)
-    got = jnp.zeros((1, LANES), F32)
+    at = lax.broadcasted_iota(jnp.int32, (1, n_rows), 1) - (me_i * 2 * half + me_j * CAP)
+    row = lax.broadcasted_iota(jnp.int32, (half, 1), 0)
+    got = jnp.zeros((half, 1), F32)
     for e in range(n_ep):
-        for s in range(CAP):
-            value = jnp.sum(
-                jnp.where(lane == me_j * CAP + s, dp_r[e], 0.0), axis=1, keepdims=True
-            )
-            got = jnp.where(lane == e * CAP + s, value, got)
-    gp_out[...] = jnp.where(prob > 0.0, got / jnp.where(prob > 0.0, prob, 1.0), 0.0)
+        for slot in range(CAP):
+            value = jnp.sum(jnp.where(at == slot, dp_r[e], 0.0), axis=1, keepdims=True)
+            got = jnp.where(row == e * CAP + slot, value, got)
+    got = jnp.where(prob > 0.0, got / jnp.where(prob > 0.0, prob, 1.0), 0.0)
+    gp_out[...] = jnp.broadcast_to(got, gp_out.shape)
 
     def drain(c, _):
         for j in ep_peers:
@@ -332,8 +344,7 @@
         return 0
 
     lax.fori_loop(0, n_ch, drain, 0)
-    for q in range(n_q):
-        dpb_copy(q).wait_send()
+    dpb_copy().wait_send()
     for q, o in far:
         dpc_copy(q, o).wait_send()
     for j in ep_peers:
@@ -358,19 +369,21 @@
         functools.partial(main_kernel, n_edp, n_ep),
         out_shape=(
             jax.ShapeDtypeStruct((n_ch, n_edp, 2 * half, WIDE), BF16),
-            jax.ShapeDtypeStruct((rows, 3 * hid), BF16),
+            jax.ShapeDtypeStruct((3 * hid, rows), BF16),
             jax.ShapeDtypeStruct((n_ch, half, WIDE), BF16),
-            jax.ShapeDtypeStruct((tok, LANES), BF16),
-            jax.ShapeDtypeStruct((1, LANES), F32),
+            jax.ShapeDtypeStruct((half, tok), BF16),
+            jax.ShapeDtypeStruct((half, tok), F32),
         ),
-        in_specs=[vmem] * 4 + [hbm] * 3 + [vmem] * 4,
+        in_specs=[hbm] * 2 + [vmem] * 2 + [hbm] * 3 + [vmem] * 4,
         out_specs=(hbm, vmem, vmem, vmem, vmem),
         scratch_shapes=[
+            pltpu.VMEM((n_ch, tok, WIDE), BF16),
+            pltpu.VMEM((n_ch, tok, WIDE), BF16),
             pltpu.VMEM((n_ch, 3 * hid, WIDE), BF16),
             pltpu.VMEM((n_ch, n_ep, SUB * 2 * CAP, LANES), BF16),
             pltpu.VMEM((n_ch, n_ep, SUB * 2 * CAP, LANES), BF16),
             pltpu.VMEM((n_ch, n_edp, 2 * half, WIDE), BF16),
-            pltpu.VMEM((rows, 3 * hid), F32),
+            pltpu.VMEM((3 * hid, rows), F32),
             pltpu.VMEM((n_ch, n_edp, half, WIDE), BF16),
             pltpu.VMEM((n_ch, n_q, half, WIDE), BF16),
             pltpu.VMEM((n_ch, n_far, half, WIDE), BF16),
@@ -378,13 +391,13 @@
             pltpu.VMEM((n_ch, half, WIDE), F32),
             pltpu.VMEM((n_ch, n_ep, SUB * CAP, LANES), BF16),
             pltpu.VMEM((n_ch, n_ep, SUB * CAP, LANES), BF16),
-            pltpu.VMEM((n_edp, half, LANES), F32),
-            pltpu.VMEM((n_q, half, LANES), F32),
-            pltpu.VMEM((n_far, half, LANES), F32),
-            pltpu.VMEM((n_far, half, LANES), F32),
-            pltpu.VMEM((half, LANES), F32),
-            pltpu.VMEM((1, LANES), F32),
-            pltpu.VMEM((n_ep, 1, LANES), F32),
+            pltpu.VMEM((1, rows), F32),
+            pltpu.VMEM((1, rows), F32),
+            pltpu.VMEM((1, rows), F32),
+            pltpu.VMEM((n_far, 1, rows), F32),
+            pltpu.VMEM((1, rows), F32),
+            pltpu.VMEM((n_ep, 1, rows), F32),
+            dma((n_ch, 2)),
             dma((n_ch, 3)),
             dma((n_ch,)),
             dma((n_ch,)),
@@ -400,7 +413,7 @@
             dma((n_ch, n_far)),
             dma((n_ch, n_ep)),
             dma((n_ch, n_ep)),
-            dma((2, n_q)),
+            dma((2,)),
             dma((n_far,)),
             dma((n_far,)),
             dma((n_ep,)),
@@ -409,27 +422,27 @@
         compiler_params=pltpu.CompilerParams(
             collective_id=0, has_side_effects=True, vmem_limit_bytes=60 * 2**20
         ),
-    )(tokens, cotangent, gate_probs, expert_ids, w_gate, w_up, w_down, *orders)
-
-
-def grads_kernel(half, z_ref, left_ref, back_ref, live_ref, gp_ref, ids_ref, tg_ref, gg_ref, wg_ref, wu_ref, wd_ref):
+    )(tokens, cotangent, gate_probs.T.astype(F32), expert_ids.T, w_gate, w_up, w_down, *orders)
+
+
+def grads_kernel(z_ref, left_ref, back_ref, live_ref, gp_ref, ids_ref, tg_ref, gg_ref, wg_ref, wu_ref, wd_ref):
     hid = wg_ref.shape[1]
-    rows = z_ref[0].reshape(left_ref.shape[0], WIDE)
+    rows = z_ref[0].reshape(left_ref.shape[1], WIDE)
     for part, out in enumerate((wg_ref, wu_ref, wd_ref)):
-        out[0] = lax.dot_general(
-            left_ref[:, part * hid : (part + 1) * hid], rows, TN, preferred_element_type=F32
+        out[0] = jnp.dot(
+            left_ref[part * hid : (part + 1) * hid], rows, preferred_element_type=F32
         ).astype(BF16)
     live = live_ref[...]
-    tg_ref[...] = jnp.dot(live[:, :half], back_ref[0], preferred_element_type=F32).astype(BF16)
+    tg_ref[...] = lax.dot_general(live, back_ref[0], TN, preferred_element_type=F32).astype(BF16)
 
     @pl.when(pl.program_id(0) == 0)
     def _():
         ids = ids_ref[...]
-        expert = lax.broadcasted_iota(jnp.int32, live.shape, 1) // CAP
+        expert = lax.broadcasted_iota(jnp.int32, live.shape, 0) // CAP
         value = live.astype(F32) * gp_ref[...]
-        for r in range(ids.shape[1]):
-            mine = jnp.where(ids[:, r : r + 1] == expert, value, 0.0)
-            gg_ref[:, r : r + 1] = jnp.sum(mine, axis=1, keepdims=True).astype(BF16)
+        for r in range(ids.shape[0]):
+            mine = jnp.where(ids[r : r + 1] == expert, value, 0.0)
+            gg_ref[r : r + 1] = jnp.sum(mine, axis=0, keepdims=True)
 
 
 def per_device(tokens, cotangent, gate_probs, expert_ids, w_gate, w_up, w_down):
@@ -442,40 +455,42 @@
     n_ch = z.shape[0]
     tok, width = tokens.shape
     hid = w_gate.shape[1]
-    rows = left.shape[0]
+    rows = left.shape[1]
+    top = gate_probs.shape[1]
 
     def whole(shape):
         return pl.BlockSpec(shape, lambda c: (0,) * len(shape))
 
     w_spec = pl.BlockSpec((1, hid, WIDE), lambda c: (0, 0, c))
     w_shape = jax.ShapeDtypeStruct(w_gate.shape, BF16)
-    return pl.pallas_call(
-        functools.partial(grads_kernel, half),
+    token_grad, gate_grad, *weight_grads = pl.pallas_call(
+        grads_kernel,
         grid=(n_ch,),
         out_shape=(
             jax.ShapeDtypeStruct((tok, width), BF16),
-            jax.ShapeDtypeStruct(gate_probs.shape, BF16),
+            jax.ShapeDtypeStruct((top, tok), F32),
             w_shape,
             w_shape,
             w_shape,
         ),
         in_specs=[
             pl.BlockSpec((1, n_edp, 2 * half, WIDE), lambda c: (c, 0, 0, 0)),
-            whole((rows, 3 * hid)),
+            whole((3 * hid, rows)),
             pl.BlockSpec((1, half, WIDE), lambda c: (c, 0, 0)),
-            whole((tok, LANES)),
-            whole((1, LANES)),
-            whole(expert_ids.shape),
+            whole((half, tok)),
+            whole((half, tok)),
+            whole((top, tok)),
         ],
         out_specs=(
             pl.BlockSpec((tok, WIDE), lambda c: (0, c)),
-            whole(gate_probs.shape),
+            whole((top, tok)),
             w_spec,
             w_spec,
             w_spec,
         ),
-        compiler_params=pltpu.CompilerParams(vmem_limit_bytes=48 * 2**20),
-    )(z, left, back, live, gp, expert_ids)
+        compiler_params=pltpu.CompilerParams(vmem_limit_bytes=63 * 2**20),
+    )(z, left, back, live, gp, expert_ids.T)
+    return (token_grad, gate_grad.T.astype(BF16), *weight_grads)
 
 
 def solution(mesh):

time: 70.6 us -> 64.1 us (0.908)
  local copies, waits for them, and re-layouts: 8.39 us -> 0 us
  other arithmetic: 0 us -> 2.54 us
    unnamed x14 -> x0, local copies, waits for them, and re-layouts: 7.72 us -> none
    convert_element_type x0 -> x2, other arithmetic: none -> 2.54 us  [the longest x1 1.28 us: exchange(): gate_probs.T.astype(F32)]
    pallas_call x1, Pallas kernels: 53.6 us -> 52.5 us  [exchange(): pl.pallas_call(functools.partial(main_kernel, n_edp, n_ep), out_shape=(ja...]
where the time goes in v2:
time: 64.1 us; the launch traced here: 63.8 us
  Pallas kernels  60.7 us (95%)
  other arithmetic  2.54 us (4%)
    pallas_call x1, Pallas kernels, exchange(): pl.pallas_call(functools.partial(main_kernel, n_edp, n_ep), out_shape=(ja...  52.5 us
    pallas_call x1, Pallas kernels, per_device(): pl.pallas_call(grads_kernel, grid=(n_ch,), out_shape=(jax.ShapeDtypeStruc...  8.17 us

profile of v2, /device:TPU:0, one launch (start us, length us, event | category | flops | bytes accessed | tf_op | source)
XLA Modules:
  0.0 63.8 jit_solution(11626416301571115470)
XLA Ops:
  0.6 1.3 %convert_bitcast_fusion.probs_ref = f32[6,128]{1,0:T(8,128)} fusion(bf16[128,6]{0,1:T(8,128)(2,1)} %param.13), kind=kLoop, calls=%fused_computation | loop fusion | flops 768 | bytes 4608 | tf_op jit(solution)/shard_map/convert_element_type | solution.py:425
  1.9 52.5 %shard_map.146 = (bf16[5,4,48,1024]{3,2,1,0:T(8,128)(2,1)}, bf16[1152,192]{1,0:T(8,128)(2,1)}, bf16[5,24,1024]{2,1,0:T(8,128)(2,1)}, bf16[24,128]{1,0:T(8,128)(2,1)}, f32[24,128]{1,0:T(8,128)}) custom-call(bf16[128,5120]{1,0:T(8,128)(2,1)} %tok_ref.1, bf16[128,5120]{1,0:T(8,128)(2,1)} %cot_ref.1, f32[6,128]{1,0:T(8,128)} %convert_bitcast_fusion.probs_ref, ...), custom_call_target="tpu_custom_call" | custom-call | tf_op jit(solution)/shard_map/pallas_call | solution.py:368
  54.4 8.2 %shard_map.147 = (bf16[128,5120]{1,0:T(8,128)(2,1)}, f32[6,128]{1,0:T(8,128)}, bf16[1,384,5120]{2,1,0:T(8,128)(2,1)}, bf16[1,384,5120]{2,1,0:T(8,128)(2,1)}, bf16[1,384,5120]{2,1,0:T(8,128)(2,1)}) custom-call(bf16[5,4,48,1024]{3,2,1,0:T(8,128)(2,1)} %get-tuple-element.15.z_ref, bf16[1152,192]{1,0:T(8,128)(2,1)} %get-tuple-element.16.left_ref, ...), custom_call_target="tpu_custom_call" | custom-call | tf_op jit(solution)/shard_map/pallas_call | solution.py:466
  62.6 1.3 %convert_bitcast_fusion.1 = bf16[128,6]{0,1:T(8,128)(2,1)} fusion(f32[6,128]{1,0:T(8,128)} %get-tuple-element.21), kind=kLoop, calls=%fused_computation.1 | loop fusion | flops 768 | bytes 4608 | tf_op jit(solution)/shard_map/convert_element_type | solution.py:493

commit v3 on v2

--- a/solution.py
+++ b/solution.py
@@ -9,6 +9,7 @@
 from jax.sharding import PartitionSpec as P
 
 CAP = 3
+LEAD = 2
 SUB = 8
 LANES = 128
 WIDE = SUB * LANES
@@ -56,7 +57,7 @@
 def main_kernel(
     n_edp, n_ep,
     tok_ref, cot_ref, probs_ref, ids_ref, wg_ref, wu_ref, wd_ref, ord2_ref, ord2t_ref, ord1_ref, ord1t_ref,
-    z_out, left_out, back_out, live_out, gp_out,
+    z_out, gate_out, up_out, down_out, back_out, live_out, gg_out,
     tok, cot, w, send_a, recv_a, z, acc, send_b, recv_b, send_c, recv_c, own, send_d, recv_d,
     dp, dp_b, dp_s, dp_c, dp_d, dp_r,
     t_sem, w_sem, z_sem, loc_sem, a_ss, a_rs, e_ss, e_rs, f_ss, f_rs, b_ss, b_rs, c_ss, c_rs, d_ss, d_rs,
@@ -99,7 +100,7 @@
         pl.semaphore_signal(barrier, inc=1, device_id=(q * 2 + core, me_j), device_id_type=MESH)
     pl.semaphore_signal(barrier, inc=1, device_id=(mate, me_j), device_id_type=MESH)
 
-    live, scaled = routes(ids_ref[...], probs_ref[...], half)
+    live, scaled = routes(ids_ref[...], probs_ref[...].astype(F32), half)
     live_out[...] = live.astype(BF16)
     live_t = live.astype(BF16)
     scaled_t = scaled.astype(BF16)
@@ -118,7 +119,7 @@
     def a_own(c):
         return pltpu.make_async_copy(send_a.at[c, me_j], recv_a.at[c, me_j], loc_sem.at[c])
 
-    def pack(c, _):
+    def pack(c):
         t_copy(c, 0).wait()
         t_copy(c, 1).wait()
         x = jnp.dot(live_t, tok[c], preferred_element_type=F32)
@@ -135,9 +136,7 @@
         a_own(c).start()
         for part in range(3):
             w_copy(c, part).start()
-        return 0
-
-    lax.fori_loop(0, n_ch, pack, 0)
+
 
     def e_copy(c, i, slot, o):
         return remote(z.at[c, me_i], z.at[c, slot], e_ss.at[c, o], e_rs.at[c, o], i, me_j)
@@ -148,7 +147,11 @@
     def gather(t, _):
         @pl.when(t < n_ch)
         def _():
-            c = t
+            pack(t)
+
+        @pl.when((t >= LEAD) & (t < n_ch + LEAD))
+        def _():
+            c = t - LEAD
             for j in ep_peers:
                 a_copy(c, j, j).wait_recv()
             a_own(c).wait()
@@ -162,17 +165,17 @@
                 e_copy(c, q * 2 + core, me_i, o).start()
             e_copy(c, mate, me_i, 0).start()
 
-        @pl.when((t >= 1) & (t < n_ch + 1))
-        def _():
-            c = t - 1
+        @pl.when((t >= LEAD + 1) & (t < n_ch + LEAD + 1))
+        def _():
+            c = t - LEAD - 1
             for _, o in far:
                 from_q = lax.rem(q_me - o + n_q, n_q)
                 e_copy(c, from_q * 2 + core, from_q * 2 + core, o).wait_recv()
                 f_copy(c, from_q * 2 + core, o).start()
 
-        @pl.when(t >= 2)
-        def _():
-            c = t - 2
+        @pl.when(t >= LEAD + 2)
+        def _():
+            c = t - LEAD - 2
             e_copy(c, mate, mate, 0).wait_recv()
             for _, o in far:
                 from_q = lax.rem(q_me - o + n_q, n_q)
@@ -192,10 +195,12 @@
 
         return 0
 
-    lax.fori_loop(0, n_ch + 2, gather, 0)
+    lax.fori_loop(0, n_ch + LEAD + 2, gather, 0)
 
     def z_copy(c):
-        return pltpu.make_async_copy(z.at[c], z_out.at[c], z_sem.at[c])
+        return pltpu.make_async_copy(
+            z.at[c], z_out.at[:, :, pl.ds(pl.multiple_of(c * WIDE, WIDE), WIDE)], z_sem.at[c]
+        )
 
     def z_start(c, _):
         z_copy(c).start()
@@ -217,7 +222,10 @@
     acc[hid : 2 * hid] = d_u
     acc[2 * hid :] = jnp.where(is_x, h, 0.0)
     dp[...] = jnp.sum(jnp.where(is_x, h * g, 0.0), axis=0, keepdims=True)
-    both = acc[: 2 * hid].T.astype(BF16)
+    turned = acc[: 2 * hid].T
+    both = jnp.concatenate(
+        [turned[i * 2 * half : (i * 2 + 1) * half] for i in range(n_edp)], axis=0
+    ).astype(BF16)
 
     def b_copy(c, q):
         return remote(
@@ -249,7 +257,7 @@
             c = t
             part = jnp.dot(both, w[c, : 2 * hid, :], preferred_element_type=F32)
             for i in range(n_edp):
-                send_b[c, i] = part[i * 2 * half : (i * 2 + 1) * half].astype(BF16)
+                send_b[c, i] = part[i * half : (i + 1) * half].astype(BF16)
             for q in range(n_q):
                 b_copy(c, q).start()
 
@@ -303,8 +311,9 @@
     lax.fori_loop(0, n_ch + 2, give_back, 0)
 
     spin = pltpu.roll(acc[2 * hid :], half, 1)
-    left_out[: 2 * hid] = acc[: 2 * hid].astype(BF16)
-    left_out[2 * hid :] = spin.astype(BF16)
+    gate_out[...] = acc[:hid].astype(BF16)
+    up_out[...] = acc[hid : 2 * hid].astype(BF16)
+    down_out[...] = spin.astype(BF16)
 
     def finish(c, _):
         for j in ep_peers:
@@ -312,7 +321,7 @@
         mixed = recv_d[c].reshape(ord1_ref.shape[0], LANES)
         rows = jnp.dot(ord1t_ref[...], mixed, preferred_element_type=F32)
         wide = jnp.concatenate([rows[k * half : (k + 1) * half] for k in range(SUB)], axis=1)
-        back_out[c] = wide.astype(BF16)
+        back_out[:, pl.ds(pl.multiple_of(c * WIDE, WIDE), WIDE)] = wide.astype(BF16)
         return 0
 
     lax.fori_loop(0, n_ch, finish, 0)
@@ -327,7 +336,14 @@
             value = jnp.sum(jnp.where(at == slot, dp_r[e], 0.0), axis=1, keepdims=True)
             got = jnp.where(row == e * CAP + slot, value, got)
     got = jnp.where(prob > 0.0, got / jnp.where(prob > 0.0, prob, 1.0), 0.0)
-    gp_out[...] = jnp.broadcast_to(got, gp_out.shape)
+    got = got.astype(BF16).astype(F32)
+    value = live * got
+    owner = lax.broadcasted_iota(jnp.int32, live.shape, 0) // CAP
+    grads = []
+    for r in range(ids_ref.shape[0]):
+        mine = jnp.where(ids_ref[r : r + 1] == owner, value, 0.0)
+        grads.append(jnp.sum(mine, axis=0, keepdims=True))
+    gg_out[...] = jnp.concatenate(grads, axis=0).astype(BF16)
 
     def drain(c, _):
         for j in ep_peers:
@@ -365,17 +381,20 @@
     hbm = pl.BlockSpec(memory_space=pl.ANY)
     dma = pltpu.SemaphoreType.DMA
     rows = n_edp * 2 * half
+    left = jax.ShapeDtypeStruct((hid, rows), BF16)
     return pl.pallas_call(
         functools.partial(main_kernel, n_edp, n_ep),
         out_shape=(
-            jax.ShapeDtypeStruct((n_ch, n_edp, 2 * half, WIDE), BF16),
-            jax.ShapeDtypeStruct((3 * hid, rows), BF16),
-            jax.ShapeDtypeStruct((n_ch, half, WIDE), BF16),
+            jax.ShapeDtypeStruct((n_edp, 2 * half, width), BF16),
+            left,
+            left,
+            left,
+            jax.ShapeDtypeStruct((half, width), BF16),
             jax.ShapeDtypeStruct((half, tok), BF16),
-            jax.ShapeDtypeStruct((half, tok), F32),
+            jax.ShapeDtypeStruct((gate_probs.shape[1], tok), BF16),
         ),
         in_specs=[hbm] * 2 + [vmem] * 2 + [hbm] * 3 + [vmem] * 4,
-        out_specs=(hbm, vmem, vmem, vmem, vmem),
+        out_specs=(hbm,) + (vmem,) * 6,
         scratch_shapes=[
             pltpu.VMEM((n_ch, tok, WIDE), BF16),
             pltpu.VMEM((n_ch, tok, WIDE), BF16),
@@ -422,75 +441,22 @@
         compiler_params=pltpu.CompilerParams(
             collective_id=0, has_side_effects=True, vmem_limit_bytes=60 * 2**20
         ),
-    )(tokens, cotangent, gate_probs.T.astype(F32), expert_ids.T, w_gate, w_up, w_down, *orders)
-
-
-def grads_kernel(z_ref, left_ref, back_ref, live_ref, gp_ref, ids_ref, tg_ref, gg_ref, wg_ref, wu_ref, wd_ref):
-    hid = wg_ref.shape[1]
-    rows = z_ref[0].reshape(left_ref.shape[1], WIDE)
-    for part, out in enumerate((wg_ref, wu_ref, wd_ref)):
-        out[0] = jnp.dot(
-            left_ref[part * hid : (part + 1) * hid], rows, preferred_element_type=F32
-        ).astype(BF16)
-    live = live_ref[...]
-    tg_ref[...] = lax.dot_general(live, back_ref[0], TN, preferred_element_type=F32).astype(BF16)
-
-    @pl.when(pl.program_id(0) == 0)
-    def _():
-        ids = ids_ref[...]
-        expert = lax.broadcasted_iota(jnp.int32, live.shape, 0) // CAP
-        value = live.astype(F32) * gp_ref[...]
-        for r in range(ids.shape[0]):
-            mine = jnp.where(ids[r : r + 1] == expert, value, 0.0)
-            gg_ref[r : r + 1] = jnp.sum(mine, axis=0, keepdims=True)
+    )(tokens, cotangent, gate_probs.T, expert_ids.T, w_gate, w_up, w_down, *orders)
 
 
 def per_device(tokens, cotangent, gate_probs, expert_ids, w_gate, w_up, w_down):
     n_edp = lax.axis_size("edp")
     n_ep = lax.axis_size("ep")
-    half = n_ep * CAP
-    z, left, back, live, gp = exchange(
+    z, gate_left, up_left, down_left, back, live, gate_grad = exchange(
         n_edp, n_ep, tokens, cotangent, gate_probs, expert_ids, w_gate, w_up, w_down
     )
-    n_ch = z.shape[0]
-    tok, width = tokens.shape
-    hid = w_gate.shape[1]
-    rows = left.shape[1]
-    top = gate_probs.shape[1]
-
-    def whole(shape):
-        return pl.BlockSpec(shape, lambda c: (0,) * len(shape))
-
-    w_spec = pl.BlockSpec((1, hid, WIDE), lambda c: (0, 0, c))
-    w_shape = jax.ShapeDtypeStruct(w_gate.shape, BF16)
-    token_grad, gate_grad, *weight_grads = pl.pallas_call(
-        grads_kernel,
-        grid=(n_ch,),
-        out_shape=(
-            jax.ShapeDtypeStruct((tok, width), BF16),
-            jax.ShapeDtypeStruct((top, tok), F32),
-            w_shape,
-            w_shape,
-            w_shape,
-        ),
-        in_specs=[
-            pl.BlockSpec((1, n_edp, 2 * half, WIDE), lambda c: (c, 0, 0, 0)),
-            whole((3 * hid, rows)),
-            pl.BlockSpec((1, half, WIDE), lambda c: (c, 0, 0)),
-            whole((half, tok)),
-            whole((half, tok)),
-            whole((top, tok)),
-        ],
-        out_specs=(
-            pl.BlockSpec((tok, WIDE), lambda c: (0, c)),
-            whole((top, tok)),
-            w_spec,
-            w_spec,
-            w_spec,
-        ),
-        compiler_params=pltpu.CompilerParams(vmem_limit_bytes=63 * 2**20),
-    )(z, left, back, live, gp, expert_ids.T)
-    return (token_grad, gate_grad.T.astype(BF16), *weight_grads)
+    rows = z.reshape(-1, z.shape[-1])
+    weight_grads = [
+        jnp.dot(left, rows, preferred_element_type=F32).astype(BF16)[None]
+        for left in (gate_left, up_left, down_left)
+    ]
+    token_grad = lax.dot_general(live, back, TN, preferred_element_type=F32).astype(BF16)
+    return (token_grad, gate_grad.T, *weight_grads)
 
 
 def solution(mesh):

time: 64.1 us -> 65.7 us (1.025)
  matrix products: 0 us -> 12.7 us
  Pallas kernels: 60.7 us -> 51.6 us
  other arithmetic: 2.54 us -> 0 us
    dot_general x0 -> x4, matrix products: none -> 12.7 us  [the longest x3 11.1 us: per_device(): jnp.dot(left, rows, preferred_element_type=F32).astype(BF16)[None]]
    pallas_call x1 -> x0, Pallas kernels: 8.17 us -> none  [per_device(): pl.pallas_call(grads_kernel, grid=(n_ch,), out_shape=(jax.ShapeDtypeStruc...]
    convert_element_type x2 -> x0, other arithmetic: 2.54 us -> none  [the longest x1 1.28 us: exchange(): gate_probs.T.astype(F32)]
    pallas_call x1, Pallas kernels: 52.5 us -> 51.6 us  [exchange(): pl.pallas_call(functools.partial(main_kernel, n_edp, n_ep), out_shape=(ja...]
where the time goes in v3:
time: 65.7 us; the launch traced here: 65.6 us
  Pallas kernels  51.6 us (79%)
  matrix products  12.7 us (19%)
  between operations  0.67 us (1%)
    pallas_call x1, Pallas kernels, exchange(): pl.pallas_call(functools.partial(main_kernel, n_edp, n_ep), out_shape=(ja...  51.6 us
    dot_general x3, matrix products, per_device(): jnp.dot(left, rows, preferred_element_type=F32).astype(BF16)[None]  11.1 us
    dot_general x1, matrix products, per_device(): lax.dot_general(live, back, TN, preferred_element_type=F32).astype(BF16)  1.59 us

profile of v3, /device:TPU:0, one launch (start us, length us, event | category | flops | bytes accessed | tf_op | source)
XLA Modules:
  0.0 65.6 jit_solution(9635100618021295658)
XLA Ops:
  0.6 51.6 %shard_map.146 = (bf16[4,48,5120]{2,1,0:T(8,128)(2,1)}, bf16[384,192]{1,0:T(8,128)(2,1)}, bf16[384,192]{1,0:T(8,128)(2,1)}, bf16[384,192]{1,0:T(8,128)(2,1)}, bf...) custom-call(bf16[128,5120]{1,0:T(8,128)(2,1)} %tok_ref.1, bf16[128,5120]{1,0:T(8,128)(2,1)} %cot_ref.1, ...), custom_call_target="tpu_custom_call" | custom-call | tf_op jit(solution)/shard_map/pallas_call | solution.py:385
  52.3 0.0 copy-start
  52.3 0.0 copy-start.2
  52.3 4.9 %fusion.1 = bf16[1,384,5120]{2,1,0:T(8,128)(2,1)} fusion(bf16[384,192]{1,0:T(8,128)(2,1)} %get-tuple-element.17, bf16[192,5120]{1,0:T(8,128)(2,1)} %bitcast.18), kind=kOutput, calls=%fused_computation.4 | convolution fusion | flops 756940800 | bytes 6045696 | tf_op jit(solution)/shard_map/dot_general | solution.py:455
  57.2 0.0 copy-done
  57.2 0.0 copy-done.2
  57.2 0.0 copy-start.1
  57.2 3.1 %fusion.2 = bf16[1,384,5120]{2,1,0:T(8,128)(2,1)} fusion(bf16[384,192]{1,0:T(8,128)(2,1)S(1)} %copy-done.2, bf16[192,5120]{1,0:T(8,128)(2,1)S(1)} %bitcast.19), kind=kOutput, calls=%fused_computation.5 | convolution fusion | flops 756940800 | bytes 6045696 | tf_op jit(solution)/shard_map/dot_general | solution.py:455
  60.3 0.0 copy-done.1
  60.3 0.0 copy-start.3
  60.3 0.0 copy-start.4
  60.3 0.0 copy-start.5
  60.3 3.1 %fusion = bf16[1,384,5120]{2,1,0:T(8,128)(2,1)} fusion(bf16[384,192]{1,0:T(8,128)(2,1)S(1)} %copy-done.1, bf16[192,5120]{1,0:T(8,128)(2,1)S(1)} %bitcast.20), kind=kOutput, calls=%fused_computation.3 | convolution fusion | flops 756940800 | bytes 6045696 | tf_op jit(solution)/shard_map/dot_general | solution.py:455
  63.4 0.0 copy-done.3
  63.4 0.0 copy-done.4
  63.4 1.6 %convolution_convert_fusion.3 = bf16[128,5120]{1,0:T(8,128)(2,1)} fusion(bf16[24,128]{1,0:T(8,128)(2,1)S(1)} %copy-done.4, bf16[24,5120]{1,0:T(8,128)(2,1)S(1)} %copy-done.3), kind=kOutput, calls=%fused_computation.6 | convolution fusion | flops 32112640 | bytes 1562624 | tf_op jit(solution)/shard_map/dot_general | solution.py:458
  65.0 0.0 copy-done.5
  65.0 0.6 copy.17
Async XLA Ops:
  52.3 4.9 %copy-start = (bf16[4,48,5120]{2,1,0:T(8,128)(2,1)S(1)}, bf16[4,48,5120]{2,1,0:T(8,128)(2,1)}, u32[]{:S(2)}) copy-start(bf16[4,48,5120]{2,1,0:T(8,128)(2,1)} %get-tuple-element.16) | copy-start | bytes 5898244
  52.3 4.9 %copy-start.2 = (bf16[384,192]{1,0:T(8,128)(2,1)S(1)}, bf16[384,192]{1,0:T(8,128)(2,1)}, u32[]{:S(2)}) copy-start(bf16[384,192]{1,0:T(8,128)(2,1)} %get-tuple-element.18) | copy-start | bytes 442372
  57.2 3.1 %copy-start.1 = (bf16[384,192]{1,0:T(8,128)(2,1)S(1)}, bf16[384,192]{1,0:T(8,128)(2,1)}, u32[]{:S(2)}) copy-start(bf16[384,192]{1,0:T(8,128)(2,1)} %get-tuple-element.15) | copy-start | bytes 442372
  60.3 3.1 %copy-start.3 = (bf16[24,5120]{1,0:T(8,128)(2,1)S(1)}, bf16[24,5120]{1,0:T(8,128)(2,1)}, u32[]{:S(2)}) copy-start(bf16[24,5120]{1,0:T(8,128)(2,1)} %get-tuple-element.13) | copy-start | bytes 737284
  60.3 3.1 %copy-start.4 = (bf16[24,128]{1,0:T(8,128)(2,1)S(1)}, bf16[24,128]{1,0:T(8,128)(2,1)}, u32[]{:S(2)}) copy-start(bf16[24,128]{1,0:T(8,128)(2,1)} %get-tuple-element.12) | copy-start | bytes 18436
  60.3 4.7 %copy-start.5 = (bf16[6,128]{1,0:T(8,128)(2,1)S(1)}, bf16[6,128]{1,0:T(8,128)(2,1)}, u32[]{:S(2)}) copy-start(bf16[6,128]{1,0:T(8,128)(2,1)} %get-tuple-element.14) | copy-start | bytes 4612

commit v4 on v3

--- a/solution.py
+++ b/solution.py
@@ -9,7 +9,9 @@
 from jax.sharding import PartitionSpec as P
 
 CAP = 3
-LEAD = 2
+LEAD = 3
+NEAR = LEAD + 2
+LAST = NEAR + 1
 SUB = 8
 LANES = 128
 WIDE = SUB * LANES
@@ -165,17 +167,17 @@
                 e_copy(c, q * 2 + core, me_i, o).start()
             e_copy(c, mate, me_i, 0).start()
 
-        @pl.when((t >= LEAD + 1) & (t < n_ch + LEAD + 1))
-        def _():
-            c = t - LEAD - 1
+        @pl.when((t >= NEAR) & (t < n_ch + NEAR))
+        def _():
+            c = t - NEAR
             for _, o in far:
                 from_q = lax.rem(q_me - o + n_q, n_q)
                 e_copy(c, from_q * 2 + core, from_q * 2 + core, o).wait_recv()
                 f_copy(c, from_q * 2 + core, o).start()
 
-        @pl.when(t >= LEAD + 2)
-        def _():
-            c = t - LEAD - 2
+        @pl.when(t >= LAST)
+        def _():
+            c = t - LAST
             e_copy(c, mate, mate, 0).wait_recv()
             for _, o in far:
                 from_q = lax.rem(q_me - o + n_q, n_q)
@@ -195,7 +197,7 @@
 
         return 0
 
-    lax.fori_loop(0, n_ch + LEAD + 2, gather, 0)
+    lax.fori_loop(0, n_ch + LAST, gather, 0)
 
     def z_copy(c):
         return pltpu.make_async_copy(
@@ -261,9 +263,9 @@
             for q in range(n_q):
                 b_copy(c, q).start()
 
-        @pl.when((t >= 1) & (t < n_ch + 1))
-        def _():
-            c = t - 1
+        @pl.when((t >= 2) & (t < n_ch + 2))
+        def _():
+            c = t - 2
             for q in range(n_q):
                 b_copy(c, q).wait_recv()
             for q, o in far:
@@ -279,9 +281,9 @@
                 for q, o in far:
                     dpc_copy(q, o).start()
 
-        @pl.when(t >= 2)
-        def _():
-            c = t - 2
+        @pl.when(t >= 4)
+        def _():
+            c = t - 4
             total = own[c]
             for q, o in far:
                 c_copy(c, q, o).wait_recv()
@@ -308,7 +310,7 @@
 
         return 0
 
-    lax.fori_loop(0, n_ch + 2, give_back, 0)
+    lax.fori_loop(0, n_ch + 4, give_back, 0)
 
     spin = pltpu.roll(acc[2 * hid :], half, 1)
     gate_out[...] = acc[:hid].astype(BF16)
@@ -444,18 +446,62 @@
     )(tokens, cotangent, gate_probs.T, expert_ids.T, w_gate, w_up, w_down, *orders)
 
 
+def grads_kernel(z_ref, gl_ref, ul_ref, dl_ref, back_ref, live_ref, gg_ref, tg_out, gg_out, wg_out, wu_out, wd_out):
+    rows = z_ref[...].reshape(gl_ref.shape[1], z_ref.shape[2])
+    for left, out in ((gl_ref, wg_out), (ul_ref, wu_out), (dl_ref, wd_out)):
+        out[0] = jnp.dot(left[...], rows, preferred_element_type=F32).astype(BF16)
+    tg_out[...] = lax.dot_general(
+        live_ref[...], back_ref[...], TN, preferred_element_type=F32
+    ).astype(BF16)
+    gg_out[...] = gg_ref[...]
+
+
 def per_device(tokens, cotangent, gate_probs, expert_ids, w_gate, w_up, w_down):
     n_edp = lax.axis_size("edp")
     n_ep = lax.axis_size("ep")
-    z, gate_left, up_left, down_left, back, live, gate_grad = exchange(
+    half = n_ep * CAP
+    results = exchange(
         n_edp, n_ep, tokens, cotangent, gate_probs, expert_ids, w_gate, w_up, w_down
     )
-    rows = z.reshape(-1, z.shape[-1])
-    weight_grads = [
-        jnp.dot(left, rows, preferred_element_type=F32).astype(BF16)[None]
-        for left in (gate_left, up_left, down_left)
-    ]
-    token_grad = lax.dot_general(live, back, TN, preferred_element_type=F32).astype(BF16)
+    tok, width = tokens.shape
+    hid = w_gate.shape[1]
+    rows = n_edp * 2 * half
+    step = WIDE // 2
+    top = gate_probs.shape[1]
+
+    def whole(*shape):
+        return pl.BlockSpec(shape, lambda c: (0,) * len(shape))
+
+    w_spec = pl.BlockSpec((1, hid, step), lambda c: (0, 0, c))
+    w_shape = jax.ShapeDtypeStruct(w_gate.shape, BF16)
+    token_grad, gate_grad, *weight_grads = pl.pallas_call(
+        grads_kernel,
+        grid=(width // step,),
+        out_shape=(
+            jax.ShapeDtypeStruct((tok, width), BF16),
+            jax.ShapeDtypeStruct((top, tok), BF16),
+            w_shape,
+            w_shape,
+            w_shape,
+        ),
+        in_specs=[
+            pl.BlockSpec((n_edp, 2 * half, step), lambda c: (0, 0, c)),
+            whole(hid, rows),
+            whole(hid, rows),
+            whole(hid, rows),
+            pl.BlockSpec((half, step), lambda c: (0, c)),
+            whole(half, tok),
+            whole(top, tok),
+        ],
+        out_specs=(
+            pl.BlockSpec((tok, step), lambda c: (0, c)),
+            whole(top, tok),
+            w_spec,
+            w_spec,
+            w_spec,
+        ),
+        compiler_params=pltpu.CompilerParams(vmem_limit_bytes=63 * 2**20),
+    )(*results)
     return (token_grad, gate_grad.T, *weight_grads)
 
 

time: 65.7 us -> 57.9 us (0.88)
  matrix products: 12.7 us -> 0 us
  Pallas kernels: 51.6 us -> 56.9 us
    dot_general x4 -> x0, matrix products: 12.7 us -> none  [the longest x3 11.1 us: per_device(): jnp.dot(left, rows, preferred_element_type=F32).astype(BF16)[None]]
    pallas_call x0 -> x1, Pallas kernels: none -> 9.89 us  [per_device(): pl.pallas_call(grads_kernel, grid=(width // step,), out_shape=(jax.ShapeD...]
    pallas_call x1, Pallas kernels: 51.6 us -> 47 us  [exchange(): pl.pallas_call(functools.partial(main_kernel, n_edp, n_ep), out_shape=(ja...]
where the time goes in v4:
time: 57.9 us; the launch traced here: 57.5 us
  Pallas kernels  56.9 us (98%)
  between operations  0.64 us (1%)
    pallas_call x1, Pallas kernels, exchange(): pl.pallas_call(functools.partial(main_kernel, n_edp, n_ep), out_shape=(ja...  47 us
    pallas_call x1, Pallas kernels, per_device(): pl.pallas_call(grads_kernel, grid=(width // step,), out_shape=(jax.ShapeD...  9.89 us

profile of v4, /device:TPU:0, one launch (start us, length us, event | category | flops | bytes accessed | tf_op | source)
XLA Modules:
  0.0 57.5 jit_solution(5413216115276332639)
XLA Ops:
  0.6 47.0 %shard_map.146 = (bf16[4,48,5120]{2,1,0:T(8,128)(2,1)}, bf16[384,192]{1,0:T(8,128)(2,1)}, bf16[384,192]{1,0:T(8,128)(2,1)}, bf16[384,192]{1,0:T(8,128)(2,1)}, bf...) custom-call(bf16[128,5120]{1,0:T(8,128)(2,1)} %tok_ref.1, bf16[128,5120]{1,0:T(8,128)(2,1)} %cot_ref.1, ...), custom_call_target="tpu_custom_call" | custom-call | tf_op jit(solution)/shard_map/pallas_call | solution.py:387
  47.6 9.9 %shard_map.147 = (bf16[128,5120]{1,0:T(8,128)(2,1)}, bf16[6,128]{1,0:T(8,128)(2,1)}, bf16[1,384,5120]{2,1,0:T(8,128)(2,1)}, bf16[1,384,5120]{2,1,0:T(8,128)(2,1)}, bf16[1,384,5120]{2,1,0:T(8,128)(2,1)}) custom-call(bf16[4,48,5120]{2,1,0:T(8,128)(2,1)} %get-tuple-element.17.z_ref, bf16[384,192]{1,0:T(8,128)(2,1)} %get-tuple-element.18.gl_ref, ...), custom_call_target="tpu_custom_call" | custom-call | tf_op jit(solution)/shard_map/pallas_call | solution.py:477

commit v5 on v4

--- a/solution.py
+++ b/solution.py
@@ -58,11 +58,11 @@
 
 def main_kernel(
     n_edp, n_ep,
-    tok_ref, cot_ref, probs_ref, ids_ref, wg_ref, wu_ref, wd_ref, ord2_ref, ord2t_ref, ord1_ref, ord1t_ref,
-    z_out, gate_out, up_out, down_out, back_out, live_out, gg_out,
-    tok, cot, w, send_a, recv_a, z, acc, send_b, recv_b, send_c, recv_c, own, send_d, recv_d,
+    tok_ref, cot_ref, probs_ref, ids_ref, wg_ref, wu_ref, wd_ref, ord2_in, ord2t_in, ord1_in, ord1t_in,
+    z_out, left_out, back_out, live_out, gg_out,
+    ord2_ref, ord2t_ref, ord1_ref, ord1t_ref, left, tok, cot, w, send_a, recv_a, z, acc, send_b, recv_b, send_c, recv_c, own, send_d, recv_d,
     dp, dp_b, dp_s, dp_c, dp_d, dp_r,
-    t_sem, w_sem, z_sem, loc_sem, a_ss, a_rs, e_ss, e_rs, f_ss, f_rs, b_ss, b_rs, c_ss, c_rs, d_ss, d_rs,
+    o_sem, l_sem, t_sem, w_sem, z_sem, loc_sem, a_ss, a_rs, e_ss, e_rs, f_ss, f_rs, b_ss, b_rs, c_ss, c_rs, d_ss, d_rs,
     pb_s, pc_ss, pc_rs, pd_ss, pd_rs,
 ):
     n_ch = z.shape[0]
@@ -89,9 +89,17 @@
             src.at[:, pl.ds(pl.multiple_of(c * WIDE, WIDE), WIDE)], dst.at[c], t_sem.at[c, part]
         )
 
+    o_copies = [
+        pltpu.make_async_copy(src, dst, o_sem.at[k])
+        for k, (src, dst) in enumerate(
+            ((ord2_in, ord2_ref), (ord2t_in, ord2t_ref), (ord1_in, ord1_ref), (ord1t_in, ord1t_ref))
+        )
+    ]
     for c in range(n_ch):
         t_copy(c, 0).start()
         t_copy(c, 1).start()
+        if c < len(o_copies):
+            o_copies[c].start()
 
     barrier = pltpu.get_barrier_semaphore()
     ep_peers = [lax.rem(me_j + o, n_ep) for o in range(1, n_ep)]
@@ -108,6 +116,8 @@
     scaled_t = scaled.astype(BF16)
     prob = jnp.sum(scaled, axis=1, keepdims=True)
 
+    for copy in o_copies:
+        copy.wait()
     pl.semaphore_wait(barrier, n_ep - 1 + n_q - 1 + 1)
 
     def remote(src, dst, ss, rs, i, j):
@@ -313,9 +323,10 @@
     lax.fori_loop(0, n_ch + 4, give_back, 0)
 
     spin = pltpu.roll(acc[2 * hid :], half, 1)
-    gate_out[...] = acc[:hid].astype(BF16)
-    up_out[...] = acc[hid : 2 * hid].astype(BF16)
-    down_out[...] = spin.astype(BF16)
+    left[: 2 * hid] = acc[: 2 * hid].astype(BF16)
+    left[2 * hid :] = spin.astype(BF16)
+    left_copy = pltpu.make_async_copy(left, left_out, l_sem)
+    left_copy.start()
 
     def finish(c, _):
         for j in ep_peers:
@@ -362,6 +373,7 @@
         return 0
 
     lax.fori_loop(0, n_ch, drain, 0)
+    left_copy.wait()
     dpb_copy().wait_send()
     for q, o in far:
         dpc_copy(q, o).wait_send()
@@ -383,21 +395,21 @@
     hbm = pl.BlockSpec(memory_space=pl.ANY)
     dma = pltpu.SemaphoreType.DMA
     rows = n_edp * 2 * half
-    left = jax.ShapeDtypeStruct((hid, rows), BF16)
+    left = jax.ShapeDtypeStruct((3 * hid, rows), BF16)
     return pl.pallas_call(
         functools.partial(main_kernel, n_edp, n_ep),
         out_shape=(
             jax.ShapeDtypeStruct((n_edp, 2 * half, width), BF16),
             left,
-            left,
-            left,
             jax.ShapeDtypeStruct((half, width), BF16),
             jax.ShapeDtypeStruct((half, tok), BF16),
             jax.ShapeDtypeStruct((gate_probs.shape[1], tok), BF16),
         ),
-        in_specs=[hbm] * 2 + [vmem] * 2 + [hbm] * 3 + [vmem] * 4,
-        out_specs=(hbm,) + (vmem,) * 6,
+        in_specs=[hbm] * 2 + [vmem] * 2 + [hbm] * 7,
+        out_specs=(hbm,) * 2 + (vmem,) * 3,
         scratch_shapes=[
+            *[pltpu.VMEM(m.shape, BF16) for m in orders],
+            pltpu.VMEM((3 * hid, rows), BF16),
             pltpu.VMEM((n_ch, tok, WIDE), BF16),
             pltpu.VMEM((n_ch, tok, WIDE), BF16),
             pltpu.VMEM((n_ch, 3 * hid, WIDE), BF16),
@@ -418,6 +430,8 @@
             pltpu.VMEM((n_far, 1, rows), F32),
             pltpu.VMEM((1, rows), F32),
             pltpu.VMEM((n_ep, 1, rows), F32),
+            dma((len(orders),)),
+            dma,
             dma((n_ch, 2)),
             dma((n_ch, 3)),
             dma((n_ch,)),
@@ -446,14 +460,53 @@
     )(tokens, cotangent, gate_probs.T, expert_ids.T, w_gate, w_up, w_down, *orders)
 
 
-def grads_kernel(z_ref, gl_ref, ul_ref, dl_ref, back_ref, live_ref, gg_ref, tg_out, gg_out, wg_out, wu_out, wd_out):
-    rows = z_ref[...].reshape(gl_ref.shape[1], z_ref.shape[2])
-    for left, out in ((gl_ref, wg_out), (ul_ref, wu_out), (dl_ref, wd_out)):
-        out[0] = jnp.dot(left[...], rows, preferred_element_type=F32).astype(BF16)
-    tg_out[...] = lax.dot_general(
-        live_ref[...], back_ref[...], TN, preferred_element_type=F32
-    ).astype(BF16)
+def grads_kernel(
+    z_in, left_in, back_in, live_ref, gg_ref,
+    tg_out, gg_out, wg_out, wu_out, wd_out,
+    z, left, back, grads, token, in_sem, left_sem, out_sem,
+):
+    n_ch = z.shape[0]
+    hid = wg_out.shape[1]
+
+    def columns(c):
+        return pl.ds(c * WIDE, WIDE)
+
+    def loads(c):
+        return (
+            pltpu.make_async_copy(z_in.at[:, :, columns(c)], z.at[c], in_sem.at[c, 0]),
+            pltpu.make_async_copy(back_in.at[:, columns(c)], back.at[c], in_sem.at[c, 1]),
+        )
+
+    def stores(c):
+        outs = [
+            pltpu.make_async_copy(
+                grads.at[c, pl.ds(part * hid, hid)], out.at[0, :, columns(c)], out_sem.at[c, part]
+            )
+            for part, out in enumerate((wg_out, wu_out, wd_out))
+        ]
+        outs.append(pltpu.make_async_copy(token.at[c], tg_out.at[:, columns(c)], out_sem.at[c, 3]))
+        return outs
+
+    left_copy = pltpu.make_async_copy(left_in, left, left_sem)
+    left_copy.start()
+    for c in range(n_ch):
+        for copy in loads(c):
+            copy.start()
     gg_out[...] = gg_ref[...]
+    left_copy.wait()
+    for c in range(n_ch):
+        for copy in loads(c):
+            copy.wait()
+        rows = z[c].reshape(left.shape[1], WIDE)
+        grads[c] = jnp.dot(left[...], rows, preferred_element_type=F32).astype(BF16)
+        token[c] = lax.dot_general(
+            live_ref[...], back[c], TN, preferred_element_type=F32
+        ).astype(BF16)
+        for copy in stores(c):
+            copy.start()
+    for c in range(n_ch):
+        for copy in stores(c):
+            copy.wait()
 
 
 def per_device(tokens, cotangent, gate_probs, expert_ids, w_gate, w_up, w_down):
@@ -466,41 +519,33 @@
     tok, width = tokens.shape
     hid = w_gate.shape[1]
     rows = n_edp * 2 * half
-    step = WIDE // 2
-    top = gate_probs.shape[1]
-
-    def whole(*shape):
-        return pl.BlockSpec(shape, lambda c: (0,) * len(shape))
-
-    w_spec = pl.BlockSpec((1, hid, step), lambda c: (0, 0, c))
+    n_ch = width // WIDE
+    vmem = pl.BlockSpec(memory_space=pltpu.VMEM)
+    hbm = pl.BlockSpec(memory_space=pl.ANY)
+    dma = pltpu.SemaphoreType.DMA
     w_shape = jax.ShapeDtypeStruct(w_gate.shape, BF16)
     token_grad, gate_grad, *weight_grads = pl.pallas_call(
         grads_kernel,
-        grid=(width // step,),
         out_shape=(
             jax.ShapeDtypeStruct((tok, width), BF16),
-            jax.ShapeDtypeStruct((top, tok), BF16),
+            jax.ShapeDtypeStruct((gate_probs.shape[1], tok), BF16),
             w_shape,
             w_shape,
             w_shape,
         ),
-        in_specs=[
-            pl.BlockSpec((n_edp, 2 * half, step), lambda c: (0, 0, c)),
-            whole(hid, rows),
-            whole(hid, rows),
-            whole(hid, rows),
-            pl.BlockSpec((half, step), lambda c: (0, c)),
-            whole(half, tok),
-            whole(top, tok),
+        in_specs=[hbm, hbm, hbm, vmem, vmem],
+        out_specs=(hbm, vmem, hbm, hbm, hbm),
+        scratch_shapes=[
+            pltpu.VMEM((n_ch, n_edp, 2 * half, WIDE), BF16),
+            pltpu.VMEM((3 * hid, rows), BF16),
+            pltpu.VMEM((n_ch, half, WIDE), BF16),
+            pltpu.VMEM((n_ch, 3 * hid, WIDE), BF16),
+            pltpu.VMEM((n_ch, tok, WIDE), BF16),
+            dma((n_ch, 2)),
+            dma,
+            dma((n_ch, 4)),
         ],
-        out_specs=(
-            pl.BlockSpec((tok, step), lambda c: (0, c)),
-            whole(top, tok),
-            w_spec,
-            w_spec,
-            w_spec,
-        ),
-        compiler_params=pltpu.CompilerParams(vmem_limit_bytes=63 * 2**20),
+        compiler_params=pltpu.CompilerParams(vmem_limit_bytes=62 * 2**20),
     )(*results)
     return (token_grad, gate_grad.T, *weight_grads)
 

time: 57.9 us -> 56.2 us (0.971)
  Pallas kernels: 56.9 us -> 55.2 us
    pallas_call x1, Pallas kernels: 9.89 us -> 8.84 us  [per_device(): pl.pallas_call(grads_kernel, out_shape=(jax.ShapeDtypeStruct((tok, width)...]
    pallas_call x1, Pallas kernels: 47 us -> 46.4 us  [exchange(): pl.pallas_call(functools.partial(main_kernel, n_edp, n_ep), out_shape=(ja...]
where the time goes in v5:
time: 56.2 us; the launch traced here: 55.9 us
  Pallas kernels  55.2 us (98%)
  between operations  0.64 us (1%)
    pallas_call x1, Pallas kernels, exchange(): pl.pallas_call(functools.partial(main_kernel, n_edp, n_ep), out_shape=(ja...  46.4 us
    pallas_call x1, Pallas kernels, per_device(): pl.pallas_call(grads_kernel, out_shape=(jax.ShapeDtypeStruct((tok, width)...  8.84 us

profile of v5, /device:TPU:0, one launch (start us, length us, event | category | flops | bytes accessed | tf_op | source)
XLA Modules:
  0.0 55.9 jit_solution(503219122055699792)
XLA Ops:
  0.6 46.4 %shard_map.146 = (bf16[4,48,5120]{2,1,0:T(8,128)(2,1)}, bf16[1152,192]{1,0:T(8,128)(2,1)}, bf16[24,5120]{1,0:T(8,128)(2,1)}, bf16[24,128]{1,0:T(8,128)(2,1)}, bf16[6,128]{1,0:T(8,128)(2,1)}) custom-call(bf16[128,5120]{1,0:T(8,128)(2,1)} %tok_ref.1, bf16[128,5120]{1,0:T(8,128)(2,1)} %cot_ref.1, bf16[6,128]{1,0:T(8,128)(2,1)} %bitcast.4, s32[6,128]{1,0:T(8,128)} %bitcast.3, ...), custom_call_target="tpu_custom_call" | custom-call | tf_op jit(solution)/shard_map/pallas_call | solution.py:399
  47.0 8.8 %shard_map.147 = (bf16[128,5120]{1,0:T(8,128)(2,1)}, bf16[6,128]{1,0:T(8,128)(2,1)}, bf16[1,384,5120]{2,1,0:T(8,128)(2,1)}, bf16[1,384,5120]{2,1,0:T(8,128)(2,1)}, bf16[1,384,5120]{2,1,0:T(8,128)(2,1)}) custom-call(bf16[4,48,5120]{2,1,0:T(8,128)(2,1)} %get-tuple-element.15.z_in, bf16[1152,192]{1,0:T(8,128)(2,1)} %get-tuple-element.16.left_in, ...), custom_call_target="tpu_custom_call" | custom-call | tf_op jit(solution)/shard_map/pallas_call | solution.py:527

commit v6 on v4

--- a/solution.py
+++ b/solution.py
@@ -58,11 +58,11 @@
 
 def main_kernel(
     n_edp, n_ep,
-    tok_ref, cot_ref, probs_ref, ids_ref, wg_ref, wu_ref, wd_ref, ord2_ref, ord2t_ref, ord1_ref, ord1t_ref,
-    z_out, gate_out, up_out, down_out, back_out, live_out, gg_out,
-    tok, cot, w, send_a, recv_a, z, acc, send_b, recv_b, send_c, recv_c, own, send_d, recv_d,
+    tok_ref, cot_ref, probs_ref, ids_ref, wg_ref, wu_ref, wd_ref, ord2_in, ord2t_in, ord1_in, ord1t_in,
+    z_out, left_out, back_out, live_out, gg_out,
+    ord2_ref, ord2t_ref, ord1_ref, ord1t_ref, left, tok, cot, w, send_a, recv_a, z, acc, send_b, recv_b, send_c, recv_c, own, send_d, recv_d,
     dp, dp_b, dp_s, dp_c, dp_d, dp_r,
-    t_sem, w_sem, z_sem, loc_sem, a_ss, a_rs, e_ss, e_rs, f_ss, f_rs, b_ss, b_rs, c_ss, c_rs, d_ss, d_rs,
+    o_sem, l_sem, t_sem, w_sem, z_sem, loc_sem, a_ss, a_rs, e_ss, e_rs, f_ss, f_rs, b_ss, b_rs, c_ss, c_rs, d_ss, d_rs,
     pb_s, pc_ss, pc_rs, pd_ss, pd_rs,
 ):
     n_ch = z.shape[0]
@@ -89,9 +89,17 @@
             src.at[:, pl.ds(pl.multiple_of(c * WIDE, WIDE), WIDE)], dst.at[c], t_sem.at[c, part]
         )
 
+    o_copies = [
+        pltpu.make_async_copy(src, dst, o_sem.at[k])
+        for k, (src, dst) in enumerate(
+            ((ord2_in, ord2_ref), (ord2t_in, ord2t_ref), (ord1_in, ord1_ref), (ord1t_in, ord1t_ref))
+        )
+    ]
     for c in range(n_ch):
         t_copy(c, 0).start()
         t_copy(c, 1).start()
+        if c < len(o_copies):
+            o_copies[c].start()
 
     barrier = pltpu.get_barrier_semaphore()
     ep_peers = [lax.rem(me_j + o, n_ep) for o in range(1, n_ep)]
@@ -108,6 +116,8 @@
     scaled_t = scaled.astype(BF16)
     prob = jnp.sum(scaled, axis=1, keepdims=True)
 
+    for copy in o_copies:
+        copy.wait()
     pl.semaphore_wait(barrier, n_ep - 1 + n_q - 1 + 1)
 
     def remote(src, dst, ss, rs, i, j):
@@ -281,9 +291,9 @@
                 for q, o in far:
                     dpc_copy(q, o).start()
 
-        @pl.when(t >= 4)
-        def _():
-            c = t - 4
+        @pl.when(t >= 5)
+        def _():
+            c = t - 5
             total = own[c]
             for q, o in far:
                 c_copy(c, q, o).wait_recv()
@@ -310,12 +320,13 @@
 
         return 0
 
-    lax.fori_loop(0, n_ch + 4, give_back, 0)
+    lax.fori_loop(0, n_ch + 5, give_back, 0)
 
     spin = pltpu.roll(acc[2 * hid :], half, 1)
-    gate_out[...] = acc[:hid].astype(BF16)
-    up_out[...] = acc[hid : 2 * hid].astype(BF16)
-    down_out[...] = spin.astype(BF16)
+    left[: 2 * hid] = acc[: 2 * hid].astype(BF16)
+    left[2 * hid :] = spin.astype(BF16)
+    left_copy = pltpu.make_async_copy(left, left_out, l_sem)
+    left_copy.start()
 
     def finish(c, _):
         for j in ep_peers:
@@ -362,6 +373,7 @@
         return 0
 
     lax.fori_loop(0, n_ch, drain, 0)
+    left_copy.wait()
     dpb_copy().wait_send()
     for q, o in far:
         dpc_copy(q, o).wait_send()
@@ -383,21 +395,21 @@
     hbm = pl.BlockSpec(memory_space=pl.ANY)
     dma = pltpu.SemaphoreType.DMA
     rows = n_edp * 2 * half
-    left = jax.ShapeDtypeStruct((hid, rows), BF16)
+    left = jax.ShapeDtypeStruct((3 * hid, rows), BF16)
     return pl.pallas_call(
         functools.partial(main_kernel, n_edp, n_ep),
         out_shape=(
             jax.ShapeDtypeStruct((n_edp, 2 * half, width), BF16),
             left,
-            left,
-            left,
             jax.ShapeDtypeStruct((half, width), BF16),
             jax.ShapeDtypeStruct((half, tok), BF16),
             jax.ShapeDtypeStruct((gate_probs.shape[1], tok), BF16),
         ),
-        in_specs=[hbm] * 2 + [vmem] * 2 + [hbm] * 3 + [vmem] * 4,
-        out_specs=(hbm,) + (vmem,) * 6,
+        in_specs=[hbm] * 2 + [vmem] * 2 + [hbm] * 7,
+        out_specs=(hbm,) * 2 + (vmem,) * 3,
         scratch_shapes=[
+            *[pltpu.VMEM(m.shape, BF16) for m in orders],
+            pltpu.VMEM((3 * hid, rows), BF16),
             pltpu.VMEM((n_ch, tok, WIDE), BF16),
             pltpu.VMEM((n_ch, tok, WIDE), BF16),
             pltpu.VMEM((n_ch, 3 * hid, WIDE), BF16),
@@ -418,6 +430,8 @@
             pltpu.VMEM((n_far, 1, rows), F32),
             pltpu.VMEM((1, rows), F32),
             pltpu.VMEM((n_ep, 1, rows), F32),
+            dma((len(orders),)),
+            dma,
             dma((n_ch, 2)),
             dma((n_ch, 3)),
             dma((n_ch,)),
@@ -446,10 +460,13 @@
     )(tokens, cotangent, gate_probs.T, expert_ids.T, w_gate, w_up, w_down, *orders)
 
 
-def grads_kernel(z_ref, gl_ref, ul_ref, dl_ref, back_ref, live_ref, gg_ref, tg_out, gg_out, wg_out, wu_out, wd_out):
-    rows = z_ref[...].reshape(gl_ref.shape[1], z_ref.shape[2])
-    for left, out in ((gl_ref, wg_out), (ul_ref, wu_out), (dl_ref, wd_out)):
-        out[0] = jnp.dot(left[...], rows, preferred_element_type=F32).astype(BF16)
+def grads_kernel(z_ref, left_ref, back_ref, live_ref, gg_ref, tg_out, gg_out, wg_out, wu_out, wd_out):
+    rows = z_ref[...].reshape(left_ref.shape[1], z_ref.shape[2])
+    hid = wg_out.shape[1]
+    for part, out in enumerate((wg_out, wu_out, wd_out)):
+        out[0] = jnp.dot(
+            left_ref[part * hid : (part + 1) * hid], rows, preferred_element_type=F32
+        ).astype(BF16)
     tg_out[...] = lax.dot_general(
         live_ref[...], back_ref[...], TN, preferred_element_type=F32
     ).astype(BF16)
@@ -466,7 +483,7 @@
     tok, width = tokens.shape
     hid = w_gate.shape[1]
     rows = n_edp * 2 * half
-    step = WIDE // 2
+    step = WIDE
     top = gate_probs.shape[1]
 
     def whole(*shape):
@@ -486,9 +503,7 @@
         ),
         in_specs=[
             pl.BlockSpec((n_edp, 2 * half, step), lambda c: (0, 0, c)),
-            whole(hid, rows),
-            whole(hid, rows),
-            whole(hid, rows),
+            whole(3 * hid, rows),
             pl.BlockSpec((half, step), lambda c: (0, c)),
             whole(half, tok),
             whole(top, tok),

time: 57.9 us -> 53.7 us (0.927)
  Pallas kernels: 56.9 us -> 52.8 us
    pallas_call x1, Pallas kernels: 9.89 us -> 7.39 us  [per_device(): pl.pallas_call(grads_kernel, grid=(width // step,), out_shape=(jax.ShapeD...]
    pallas_call x1, Pallas kernels: 47 us -> 45.4 us  [exchange(): pl.pallas_call(functools.partial(main_kernel, n_edp, n_ep), out_shape=(ja...]
where the time goes in v6:
time: 53.7 us; the launch traced here: 53.4 us
  Pallas kernels  52.8 us (98%)
  between operations  0.64 us (1%)
    pallas_call x1, Pallas kernels, exchange(): pl.pallas_call(functools.partial(main_kernel, n_edp, n_ep), out_shape=(ja...  45.4 us
    pallas_call x1, Pallas kernels, per_device(): pl.pallas_call(grads_kernel, grid=(width // step,), out_shape=(jax.ShapeD...  7.39 us

profile of v6, /device:TPU:0, one launch (start us, length us, event | category | flops | bytes accessed | tf_op | source)
XLA Modules:
  0.0 53.4 jit_solution(3207480037395304565)
XLA Ops:
  0.6 45.4 %shard_map.146 = (bf16[4,48,5120]{2,1,0:T(8,128)(2,1)}, bf16[1152,192]{1,0:T(8,128)(2,1)}, bf16[24,5120]{1,0:T(8,128)(2,1)}, bf16[24,128]{1,0:T(8,128)(2,1)}, bf16[6,128]{1,0:T(8,128)(2,1)}) custom-call(bf16[128,5120]{1,0:T(8,128)(2,1)} %tok_ref.1, bf16[128,5120]{1,0:T(8,128)(2,1)} %cot_ref.1, bf16[6,128]{1,0:T(8,128)(2,1)} %bitcast.4, s32[6,128]{1,0:T(8,128)} %bitcast.3, ...), custom_call_target="tpu_custom_call" | custom-call | tf_op jit(solution)/shard_map/pallas_call | solution.py:399
  46.0 7.4 %shard_map.147 = (bf16[128,5120]{1,0:T(8,128)(2,1)}, bf16[6,128]{1,0:T(8,128)(2,1)}, bf16[1,384,5120]{2,1,0:T(8,128)(2,1)}, bf16[1,384,5120]{2,1,0:T(8,128)(2,1)}, bf16[1,384,5120]{2,1,0:T(8,128)(2,1)}) custom-call(bf16[4,48,5120]{2,1,0:T(8,128)(2,1)} %get-tuple-element.15.z_ref, bf16[1152,192]{1,0:T(8,128)(2,1)} %get-tuple-element.16.left_ref, ...), custom_call_target="tpu_custom_call" | custom-call | tf_op jit(solution)/shard_map/pallas_call | solution.py:494
